TPU v7x, 32 devices: a whole 2x2x4 slice. The times are simulated.
32 devices in a mesh: join: 16 (over z, y, x), view: 2 (over core).
Axes of the slice: x: 2, y: 2, z: 4, core: 2. Of those that a mesh axis runs over, the one named last changes fastest.
Arguments:
- estimate: float32 [64, 256, 256], P('join', 'view'), may hold values from 0.5 to 2
- views: bfloat16 [64, 6, 256, 256], P('join', None, 'view'), may hold values from 0.25 to 4
- owners: int32 [64, 6], P('join'), may hold values from 0 to 15, all different within a row; in each aligned block of 4 rows (0 to 3, 4 to 7, ...) at most 3 rows name the same one
- local_blocks: int32 [64, 6], P('join'), may hold values from 0 to 3, as said below
- psf: float32 [6, 33], replicated, may hold values from 0.05 to 1
Outputs:
- deconvolved: float32 [64, 256, 256], P('join', 'view')
Inputs may be any that keep to these rules, and one draw needn't show every extreme that they name: `owners`: each row names 6 different join indices; in the 4 rows of one join index no join index is named more than 3 times, and in every draw some join index is named exactly 3 times by some device's rows. `local_blocks`: in every draw one local block index, drawn from the seed and neither 0 nor 4 - 1, is named by no entry, so the estimate blocks with that index are imaged by no view; the other values all appear.
All inputs are finite; a program needn't handle non-finite values.
Results may differ from a plain program's by a relative error of at most 0.00065.
Values may be sent and summed in bfloat16 or wider, within the bound.
No kernel may reach another device: no remote copies, remote signals or barrier semaphores. Data moves between devices by JAX's collectives and lax.ppermute only.
A program may use at most 64 MiB of HBM per device.

v0:
```python
import functools

import jax
import jax.numpy as jnp
from jax import lax
from jax.experimental import pallas as pl
from jax.experimental.pallas import tpu as pltpu
from jax.sharding import PartitionSpec as P

H = 16
CAP = 3
MAIN = 2
ITERS = 2
GROUP = 16
TILE = 16
EST_HALO = 2 * ITERS * H
VIEW_HALO = EST_HALO - H

SMEM = pl.BlockSpec(memory_space=pltpu.SMEM)
VMEM = pl.BlockSpec(memory_space=pltpu.VMEM)
ANY = pl.BlockSpec(memory_space=pl.ANY)
HBM = pl.BlockSpec(memory_space=pltpu.HBM)


def pack_kernel(owners, blocks_of, here, views, main, *refs):
    rows, (table, seen, taken, staged, table_rows, in_sems, out_sems, table_sems) = refs[:-8], refs[-8:]
    blocks, nviews, depth, lat = views.shape
    peers, groups = seen.shape[0], len(rows)
    members = peers // groups
    pairs = [(i, v) for i in range(blocks) for v in range(nviews)]
    loads = [
        pltpu.make_async_copy(views.at[i, v], staged.at[i, v], in_sems.at[i, v]) for i, v in pairs
    ]
    for load in loads:
        load.start()

    @pl.loop(0, peers)
    def _(peer):
        seen[peer] = 0

    for group in range(groups):
        taken[group] = 0

    @pl.loop(0, peers * CAP)
    def _(slot):
        table[slot] = -1

    table[peers * CAP] = 0
    stores = []
    for (i, v), load in zip(pairs, loads):
        owner = owners[i, v]
        order = seen[owner]
        seen[owner] = order + 1
        table[owner * CAP + order] = blocks_of[i, v] * nviews + v
        away = lax.rem(owner // members + groups - here[0], groups)
        in_main = order < MAIN
        in_rows = jnp.logical_and(jnp.logical_not(in_main), taken[away] == 0)
        load.wait()

        @pl.when(in_main)
        def _():
            pltpu.make_async_copy(
                staged.at[i, v], main.at[owner * MAIN + order], out_sems.at[i, v]
            ).start()

        @pl.when(jnp.logical_not(in_main))
        def _():
            table[peers * CAP] = jnp.where(in_rows, table[peers * CAP], 1)
            for k in range(groups):

                @pl.when(jnp.logical_and(in_rows, away == k))
                def _():
                    taken[k] = 1
                    pltpu.make_async_copy(
                        staged.at[i, v], rows[k].at[0, pl.ds(0, depth)], out_sems.at[i, v]
                    ).start()

        stores.append((i, v, jnp.logical_or(in_main, in_rows)))

    lane = lax.broadcasted_iota(jnp.int32, (TILE, lat), 1)
    row = jnp.full((TILE, lat), -1, jnp.int32)
    for slot in range(peers * CAP + 1):
        row = jnp.where(lane == slot, table[slot], row)
    table_rows[...] = row.astype(jnp.float32).astype(table_rows.dtype)
    table_stores = [
        pltpu.make_async_copy(table_rows, rows[k].at[0, pl.ds(depth, TILE)], table_sems.at[k])
        for k in range(groups)
    ]
    for store in table_stores:
        store.start()
    for i, v, stored in stores:

        @pl.when(stored)
        def _():
            pltpu.make_async_copy(staged.at[i, v], main.at[0], out_sems.at[i, v]).wait()

    for store in table_stores:
        store.wait()


def pack(views, owners, blocks_of, here, peers, groups):
    blocks, nviews, depth, lat = views.shape
    assert peers * CAP < lat
    return pl.pallas_call(
        pack_kernel,
        out_shape=(jax.ShapeDtypeStruct((peers * MAIN, depth, lat), views.dtype),)
        + (jax.ShapeDtypeStruct((1, depth + TILE, lat), views.dtype),) * groups,
        in_specs=[SMEM, SMEM, SMEM, ANY],
        out_specs=(ANY,) * (1 + groups),
        scratch_shapes=[
            pltpu.SMEM((peers * CAP + 1,), jnp.int32),
            pltpu.SMEM((peers,), jnp.int32),
            pltpu.SMEM((groups,), jnp.int32),
            pltpu.VMEM(views.shape, views.dtype),
            pltpu.VMEM((TILE, lat), views.dtype),
            pltpu.SemaphoreType.DMA((blocks, nviews)),
            pltpu.SemaphoreType.DMA((blocks, nviews)),
            pltpu.SemaphoreType.DMA((groups,)),
        ],
        name="pack",
    )(owners, blocks_of, here, views)


def all_thirds_kernel(owners, views, out, seen, staged, sems):
    blocks, nviews = views.shape[0], views.shape[1]

    @pl.loop(0, out.shape[0])
    def _(peer):
        seen[peer] = 0

    for i in range(blocks):
        for v in range(nviews):
            owner = owners[i, v]
            order = seen[owner]
            seen[owner] = order + 1

            @pl.when(order >= MAIN)
            def _():
                load = pltpu.make_async_copy(views.at[i, v], staged, sems.at[0])
                load.start()
                load.wait()
                store = pltpu.make_async_copy(staged, out.at[owner], sems.at[1])
                store.start()
                store.wait()


def pack_all_thirds(views, owners, peers):
    depth, lat = views.shape[2:]
    return pl.pallas_call(
        all_thirds_kernel,
        out_shape=jax.ShapeDtypeStruct((peers, depth, lat), views.dtype),
        in_specs=[SMEM, ANY],
        out_specs=ANY,
        scratch_shapes=[
            pltpu.SMEM((peers,), jnp.int32),
            pltpu.VMEM((depth, lat), views.dtype),
            pltpu.SemaphoreType.DMA((2,)),
        ],
        name="all_thirds",
    )(owners, views)


def group_count(peers):
    members = 1
    while peers % (2 * members) == 0 and members * members < peers:
        members *= 2
    return peers // members


def along_groups(rows):
    peers = lax.axis_size("join")
    members = peers // len(rows)
    line = [rows[0]]
    for k in range(1, len(rows)):
        line.append(
            lax.ppermute(rows[k], "join", [(i, (i + k * members) % peers) for i in range(peers)])
        )
    return line


def among_members(line):
    peers = lax.axis_size("join")
    members = peers // len(line)
    line = jnp.concatenate(line, axis=0)
    parts = [line]
    for m in range(1, members):
        parts.append(lax.ppermute(line, "join", [(i, i ^ m) for i in range(peers)]))
    return parts


def sources_of_parts(groups):
    peers = lax.axis_size("join")
    members = peers // groups
    here = lax.axis_index("join")
    at = jnp.arange(peers, dtype=jnp.int32)
    group = lax.rem(here // members + groups - lax.rem(at, groups), groups)
    return group * members + jnp.bitwise_xor(lax.rem(here, members), at // groups)


def ends_kernel(start, *refs):
    blocks, (out, staged, sems) = refs[:-3], refs[-3:]
    width = out.shape[1]
    copies, first = [], 0
    for k, block in enumerate(blocks):
        number = block.shape[0]
        held = staged.at[pl.ds(first, number)]
        rows = block.at[:, pl.ds(pl.multiple_of(start[0], TILE), width)]
        copies.append(
            (
                pltpu.make_async_copy(rows, held, sems.at[0, k]),
                pltpu.make_async_copy(held, out.at[pl.ds(first, number)], sems.at[1, k]),
            )
        )
        first += number
    for load, _ in copies:
        load.start()
    for load, store in copies:
        load.wait()
        store.start()
    for _, store in copies:
        store.wait()


def ends(blocks, start, width):
    if len(blocks) == 1:
        return lax.dynamic_slice_in_dim(blocks[0], start, width, axis=1)
    shape = (sum(block.shape[0] for block in blocks), width, blocks[0].shape[2])
    return pl.pallas_call(
        ends_kernel,
        out_shape=jax.ShapeDtypeStruct(shape, blocks[0].dtype),
        in_specs=[SMEM] + [ANY] * len(blocks),
        out_specs=ANY,
        scratch_shapes=[
            pltpu.VMEM(shape, blocks[0].dtype),
            pltpu.SemaphoreType.DMA((2, len(blocks))),
        ],
        name="ends",
    )(jnp.asarray(start, jnp.int32)[None], *blocks)


def halos(blocks, depth, width):
    count = lax.axis_size("view")
    if count == 1:
        return []
    if count == 2:
        sent = ends(blocks, jnp.where(lax.axis_index("view") == 0, depth - width, 0), width)
        return [lax.ppermute(sent, "view", [(0, 1), (1, 0)])]
    forward = [(i, i + 1) for i in range(count - 1)]
    backward = [(target, source) for source, target in forward]
    low = lax.ppermute(ends(blocks, depth - width, width), "view", forward)
    high = lax.ppermute(ends(blocks, 0, width), "view", backward)
    return [low, high]


def framed(block, sides, dim):
    if not sides:
        return block
    if len(sides) == 2:
        return jnp.concatenate([sides[0], block, sides[1]], axis=dim)
    (side,) = sides
    return jnp.where(
        lax.axis_index("view") == 0,
        jnp.concatenate([block, side], axis=dim),
        jnp.concatenate([side, block], axis=dim),
    )


def low_rows():
    count = lax.axis_size("view")
    if count == 2:
        return jnp.where(lax.axis_index("view") == 0, 0, H).astype(jnp.int32)
    return jnp.int32(0 if count == 1 else H)


def halo_rows(sweep):
    return VIEW_HALO - 2 * H * sweep


def piece_starts(depth, sweep):
    count = lax.axis_size("view")
    width = halo_rows(sweep)
    if count == 1:
        return [jnp.int32(0)]
    if count == 2:
        first = lax.axis_index("view") == 0
        return [jnp.where(first, 0, width), jnp.where(first, depth, 0)]
    return [jnp.int32(width), jnp.int32(0), jnp.int32(width + depth)]


def bands_kernel(shapes, shifts, taps_rows, *refs):
    width = taps_rows.shape[-1]
    nviews = taps_rows.shape[1]

    def band(which, v, shift, rows):
        spread = jnp.broadcast_to(taps_rows[which, v : v + 1, :], (rows, width))
        return pltpu.roll(pltpu.roll(spread, 0, 1, stride=1, stride_axis=0), shift, 1)

    at = 0
    for sweep, pieces in enumerate(shapes):
        forward, mirror = refs[2 * sweep], refs[2 * sweep + 1]
        columns, outs = forward.shape[2], mirror.shape[1]
        lane = lax.broadcasted_iota(jnp.int32, (outs, width), 1)
        for v in range(nviews):
            total = jnp.zeros((outs, width), jnp.float32)
            first = 0
            for piece, rows in enumerate(pieces):
                part = band(0, v, shifts[at + 2 * piece], rows)
                forward[v, first : first + rows] = part[:, :columns].astype(forward.dtype)
                inside = jnp.logical_and(lane >= first, lane < first + rows)
                total = jnp.where(inside, band(1, v, shifts[at + 2 * piece + 1], outs), total)
                first += rows
            mirror[v] = total[:, :first].astype(mirror.dtype)
        at += 2 * len(pieces)


def bands(kernel, depth, sides):
    nviews, taps = kernel.shape
    low = low_rows()
    frame = depth + sides * EST_HALO
    width = -(-(frame + 4 * H) // 128) * 128
    shapes, shifts, outs = [], [], []
    for sweep in range(ITERS):
        pieces = (depth,) + (halo_rows(sweep),) * sides
        first = 0
        for rows, start in zip(pieces, piece_starts(depth, sweep)):
            shifts.append(lax.rem(start + low - H + width, width))
            shifts.append(lax.rem(first - start + low - H + width, width))
            first += rows
        shapes.append(pieces)
        rows_in = frame - 2 * sides * H * sweep
        outs.append(jax.ShapeDtypeStruct((nviews, first, rows_in), jnp.bfloat16))
        outs.append(jax.ShapeDtypeStruct((nviews, rows_in - 2 * sides * H, first), jnp.bfloat16))
    rows = jnp.stack([kernel, kernel[:, ::-1]]).astype(jnp.float32)
    rows = jnp.pad(rows, ((0, 0), (0, 0), (0, width - taps)))
    return pl.pallas_call(
        functools.partial(bands_kernel, shapes),
        out_shape=outs,
        in_specs=[SMEM, VMEM],
        out_specs=[VMEM] * len(outs),
        cost_estimate=pl.CostEstimate(flops=10**11, bytes_accessed=0, transcendentals=0),
        name="bands",
    )(jnp.stack(shifts).astype(jnp.int32), rows)


def list_starts(peers):
    main, third = peers * MAIN + GROUP, peers + GROUP
    return 0, main, 2 * main, 2 * main + third, 2 * main + 2 * third, 2 * main + 3 * third


def plan_kernel(nviews, blocks, place, source, *refs):
    parts, (lists, any_crowded, tables, rows, scalars, sems) = refs[:-6], refs[-6:]
    per_part, depth, lat = parts[0].shape
    depth -= TILE
    peers = source.shape[0]
    blank = blocks * nviews
    main_slot, main_code, third_slot, third_source, third_code, numbers = list_starts(peers)
    loads = [
        pltpu.make_async_copy(
            part.at[:, pl.ds(depth, TILE)], tables.at[pl.ds(j * per_part, per_part)], sems.at[j]
        )
        for j, part in enumerate(parts)
    ]
    for load in loads:
        load.start()
    lists[numbers + 2] = place[1]
    for b in range(blocks):
        lists[numbers + 3 + b] = 0
    for load in loads:
        load.wait()
    at = lax.broadcasted_iota(jnp.int32, (peers, lat), 0)
    together = jnp.zeros((peers, lat), jnp.float32)
    for t in range(peers):
        row = jnp.broadcast_to(tables[t, :1].astype(jnp.float32), (peers, lat))
        together = jnp.where(at == t, row, together)
    rows[...] = together.astype(jnp.int32)
    copy = pltpu.make_async_copy(rows, scalars, sems.at[len(parts)])
    copy.start()
    copy.wait()

    def enlist(t, carry):
        in_main, in_third, crowded = carry
        for order in range(CAP):
            code = scalars[t, place[0] * CAP + order]
            valid = code >= 0

            @pl.when(valid)
            def _():
                at = numbers + 3 + code // nviews
                lists[at] = lists[at] + 1
                if order < MAIN:
                    lists[main_slot + in_main] = source[t] * MAIN + order
                    lists[main_code + in_main] = code
                else:
                    lists[third_slot + in_third] = t
                    lists[third_source + in_third] = source[t]
                    lists[third_code + in_third] = code

            if order < MAIN:
                in_main = in_main + valid.astype(jnp.int32)
            else:
                in_third = in_third + valid.astype(jnp.int32)
        return in_main, in_third, jnp.maximum(crowded, scalars[t, peers * CAP])

    zero = jnp.int32(0)
    in_main, in_third, crowded = lax.fori_loop(0, peers, enlist, (zero, zero, zero))
    lists[numbers] = in_main
    lists[numbers + 1] = in_third
    any_crowded[0] = crowded
    for more in range(GROUP - 1):
        lists[main_slot + in_main + more] = lists[main_slot]
        lists[main_code + in_main + more] = blank
        lists[third_code + in_third + more] = blank


def plan(parts, source, here, blocks, nviews):
    peers = source.shape[0]
    lat = parts[0].shape[-1]
    length = list_starts(peers)[-1] + 3 + blocks
    return pl.pallas_call(
        functools.partial(plan_kernel, nviews, blocks),
        out_shape=(
            jax.ShapeDtypeStruct((length,), jnp.int32),
            jax.ShapeDtypeStruct((1,), jnp.int32),
        ),
        in_specs=[SMEM] * 2 + [ANY] * len(parts),
        out_specs=(SMEM,) * 2,
        scratch_shapes=[
            pltpu.VMEM((peers, TILE, lat), parts[0].dtype),
            pltpu.VMEM((peers, lat), jnp.int32),
            pltpu.SMEM((peers, lat), jnp.int32),
            pltpu.SemaphoreType.DMA((len(parts) + 1,)),
        ],
        name="plan",
    )(jnp.stack([here, low_rows()]), source, *parts)


def deconvolve_kernel(starts, nparts, sides, guard, lists, main, est, *refs):
    main_slot, main_code, third_slot, third_code, numbers = starts
    parts, third_halo, refs = refs[:nparts], refs[nparts : nparts + sides], refs[nparts + sides :]
    number = 2 * ITERS + sides
    sources, out, refs = refs[:number], refs[number], refs[number + 1 :]
    copied, refs = refs[:number], refs[number:]
    bands_of, main_halo = copied[: 2 * ITERS], copied[2 * ITERS :]
    held, recip, following, total, result, own_sems, held_sems, out_sems = refs
    blocks, depth, lat = out.shape
    nviews = bands_of[0].shape[0]
    per_part = parts[0].shape[0]
    mains, thirds = lists[numbers], lists[numbers + 1]
    low = pl.multiple_of(lists[numbers + 2], H)
    counts = [lists[numbers + 3 + b] for b in range(blocks)]
    own = [
        pltpu.make_async_copy(source, to, own_sems.at[k])
        for k, (source, to) in enumerate(zip(sources, copied))
    ]
    for copy in own:
        copy.start()

    def copies(p, part, at, slot):
        yield pltpu.make_async_copy(
            part.at[at, pl.ds(0, depth)], held.at[p, pl.ds(0, depth)], held_sems.at[p, 0]
        )
        for side, ref in enumerate(third_halo):
            rows = pl.ds(depth + side * VIEW_HALO, VIEW_HALO)
            yield pltpu.make_async_copy(ref.at[slot], held.at[p, rows], held_sems.at[p, 1 + side])

    @pl.loop(0, thirds)
    def _(p):
        slot = lists[third_slot + p]
        for j, part in enumerate(parts):

            @pl.when(jnp.logical_and(slot >= j * per_part, slot < (j + 1) * per_part))
            def _():
                for copy in copies(p, part, slot - j * per_part, slot):
                    copy.start()

    @pl.loop(thirds, (thirds + (GROUP - 1)) // GROUP * GROUP)
    def _(p):
        held[p] = jnp.zeros(held.shape[1:], held.dtype)

    recip[blocks * nviews] = jnp.zeros(recip.shape[1:], recip.dtype)
    stores = []
    for sweep in range(ITERS):
        current = est if sweep == 0 else following
        forward, mirror = bands_of[2 * sweep], bands_of[2 * sweep + 1]
        next_rows, view_rows = mirror.shape[1], mirror.shape[2]
        side_rows = halo_rows(sweep)
        next_at = pl.multiple_of(2 * low, 2 * H)
        halo_at = [pl.multiple_of(2 * sweep * low, 2 * H), 0]
        own[2 * sweep].wait()
        for b in range(blocks):

            @pl.when(counts[b] > 0)
            def _():
                rounded = current[b, : forward.shape[2]].astype(jnp.bfloat16)
                for v in range(nviews):
                    blurred = jnp.dot(forward[v], rounded, preferred_element_type=jnp.float32)
                    inverse = 1.0 / blurred
                    if guard:
                        inverse = jnp.where(blurred > 0, inverse, 0.0)
                    recip[b * nviews + v, :view_rows] = inverse

        total[:, :next_rows] = jnp.zeros((blocks + 1, next_rows, lat), jnp.float32)

        def main_rows(p):
            slot = lists[main_slot + p]
            rows = [main[slot]]
            for side, ref in enumerate(main_halo):
                rows.append(ref[slot, pl.ds(halo_at[side], side_rows)])
            return rows

        def third_rows(p):
            rows = [held[p, :depth]]
            for side in range(sides):
                at = depth + side * VIEW_HALO + halo_at[side]
                rows.append(held[p, pl.ds(pl.multiple_of(at, H), side_rows)])
            return rows

        def add(number, rows_of, code_at):
            @pl.loop(0, (number + (GROUP - 1)) // GROUP)
            def _(group):
                gained = []
                for member in range(GROUP):
                    p = group * GROUP + member
                    code = lists[code_at + p]
                    b = code // nviews
                    pieces, first = [], 0
                    for rows in rows_of(p):
                        last = first + rows.shape[0]
                        quotient = rows.astype(jnp.float32) * recip[code, first:last]
                        pieces.append(quotient.astype(jnp.bfloat16))
                        first = last
                    part = jnp.dot(
                        mirror[code - b * nviews],
                        jnp.concatenate(pieces, axis=0),
                        preferred_element_type=jnp.float32,
                    )
                    gained.append((b, part))
                for b, part in gained:
                    total[b, :next_rows] += part

        own[2 * sweep + 1].wait()
        if sweep == 0:
            for copy in own[2 * ITERS :]:
                copy.wait()
        add(mains, main_rows, main_code)
        if sweep == 0:

            @pl.loop(0, thirds)
            def _(p):
                for copy in copies(p, parts[0], 0, 0):
                    copy.wait()

        add(thirds, third_rows, third_code)
        for b in range(blocks):

            @pl.when(counts[b] > 0)
            def _():
                updated = current[b, pl.ds(next_at, next_rows)] * (
                    total[b, :next_rows] / counts[b].astype(jnp.float32)
                )
                if sweep < ITERS - 1:
                    following[b, :next_rows] = updated
                else:
                    result[b] = updated

            if sweep == ITERS - 1:

                @pl.when(counts[b] == 0)
                def _():
                    at = pl.multiple_of(2 * ITERS * low, 2 * H)
                    result[b] = est[b, pl.ds(at, depth)]

                store = pltpu.make_async_copy(result.at[b], out.at[b], out_sems.at[b])
                store.start()
                stores.append(store)
    for store in stores:
        store.wait()


def deconvolve(lists, starts, main, parts, main_halo, third_halo, est, matrices, depth, guard):
    blocks, frame, lat = est.shape
    nviews, view_rows = matrices[0].shape[:2]
    sides = len(main_halo)
    thirds = parts[0].shape[0] * len(parts) + GROUP
    following = (frame - 2 * sides * H, lat)
    copied = [*matrices, *main_halo]
    in_place = [*parts, *third_halo, *copied]
    return pl.pallas_call(
        functools.partial(deconvolve_kernel, starts, len(parts), sides, guard),
        out_shape=pltpu.HBM((blocks, depth, lat), jnp.float32),
        in_specs=[SMEM] + [VMEM] * 2 + [ANY] * len(in_place),
        out_specs=HBM,
        scratch_shapes=[pltpu.VMEM(array.shape, array.dtype) for array in copied]
        + [
            pltpu.VMEM((thirds, view_rows, lat), jnp.bfloat16),
            pltpu.VMEM((blocks * nviews + 1, view_rows, lat), jnp.float32),
            pltpu.VMEM((blocks, *following), jnp.float32),
            pltpu.VMEM((blocks + 1, *following), jnp.float32),
            pltpu.VMEM((blocks, depth, lat), jnp.float32),
            pltpu.SemaphoreType.DMA((len(copied),)),
            pltpu.SemaphoreType.DMA((thirds, 1 + sides)),
            pltpu.SemaphoreType.DMA((blocks,)),
        ],
        compiler_params=pltpu.CompilerParams(vmem_limit_bytes=24 * 1024 * 1024),
        name="deconvolve",
    )(lists, main, est, *in_place)


def local(estimate, views, owners, local_blocks, psf):
    blocks, depth, lat = estimate.shape
    nviews = views.shape[1]
    peers = lax.axis_size("join")
    groups = group_count(peers)
    here = lax.axis_index("join").astype(jnp.int32)
    normed = psf / jnp.sum(psf, axis=1, keepdims=True)
    kernel = normed.astype(jnp.bfloat16)

    packed, *rows = pack(
        views, owners, local_blocks, (here // (peers // groups))[None], peers, groups
    )
    line = along_groups(rows)
    arrived = lax.all_to_all(
        packed.reshape(peers, MAIN, depth, lat), "join", split_axis=0, concat_axis=0, tiled=True
    ).reshape(peers * MAIN, depth, lat)

    parts = among_members(line)
    source = sources_of_parts(groups)
    kernel, estimate, line = lax.optimization_barrier((kernel, estimate, line))
    est_halos = halos([estimate], depth, EST_HALO)
    est = framed(estimate, est_halos, 1)
    matrices = bands(kernel, depth, len(est_halos))
    parts, source, est, matrices = lax.optimization_barrier((parts, source, est, matrices))
    third_halo = halos(parts, depth, VIEW_HALO)
    planned = plan(parts, source, here, blocks, nviews)
    arrived, parts, third_halo, planned, est, matrices = lax.optimization_barrier(
        (arrived, parts, third_halo, planned, est, matrices)
    )
    lists, any_crowded = planned
    main_slot, main_code, third_slot, third_source, third_code, numbers = list_starts(peers)

    main_halo = halos([arrived], depth, VIEW_HALO)
    guard = lax.axis_size("view") > 2

    def finish(third_at, thirds, third_halo):
        return deconvolve(
            lists,
            (main_slot, main_code, third_at, third_code, numbers),
            arrived,
            thirds,
            main_halo,
            third_halo,
            est,
            matrices,
            depth,
            guard,
        )

    def fallback():
        sent = pack_all_thirds(views, owners, peers)
        thirds = lax.all_to_all(sent, "join", split_axis=0, concat_axis=0, tiled=True)
        return finish(third_source, [thirds], halos([thirds], depth, VIEW_HALO))

    return lax.cond(
        any_crowded[0] > 0, fallback, lambda: finish(third_slot, parts, third_halo)
    )


def solution(mesh):
    in_specs = (
        P("join", "view", None),
        P("join", None, "view", None),
        P("join", None),
        P("join", None),
        P(),
    )
    out_specs = P("join", "view", None)
    return jax.shard_map(local, mesh=mesh, in_specs=in_specs, out_specs=out_specs, check_vma=False)
```

profile of v0, /device:TPU:13, one launch (start us, length us, event | category | flops | bytes accessed | tf_op | source)
XLA Modules:
  0.0 69.7 jit_solution(10944853683378156054)
XLA Ops:
  0.0 3.3 %pack.1 = (bf16[32,128,256]{2,1,0:T(8,128)(2,1)}, bf16[1,144,256]{2,1,0:T(8,128)(2,1)}, bf16[1,144,256]{2,1,0:T(8,128)(2,1)}, bf16[1,144,256]{2,1,0:T(8,128)(2,1)}, bf16[1,144,256]{2,1,0:T(8,128)(2,1)}) custom-call(s32[4,6]{1,0:T(4,128)} %owners.1, s32[4,6]{1,0:T(4,128)} %blocks_of.1, s32[1]{0:T(128)} %bitcast.here, bf16[4,6,128,256]{3,2,1,0:T(8,128)(2,1)} %views.1), custom_call_target="tpu_custom_call" | custom-call | tf_op jit(solution)/shard_map/pack/pallas_call | solution.py:104
  3.3 1.3 %collective-permute-start.1 = (bf16[1,144,256]{2,1,0:T(8,128)(2,1)}, bf16[1,144,256]{2,1,0:T(8,128)(2,1)S(1)}, u32[]{:S(2)}, u32[]{:S(2)}) collective-permute-start(bf16[1,144,256]{2,1,0:T(8,128)(2,1)} %get-tuple-element.115), channel_id=1, source_target_pairs={{0,8},{2,10},{4,12},{6,14},{8,16},{10,18},{12,20},{14,22},{16,24},... | collective-permute-start | bytes 221192 | tf_op jit(solution)/shard_map/ppermute | solution.py:176
  4.6 1.2 %collective-permute-start.2 = (bf16[1,144,256]{2,1,0:T(8,128)(2,1)}, bf16[1,144,256]{2,1,0:T(8,128)(2,1)S(1)}, u32[]{:S(2)}, u32[]{:S(2)}) collective-permute-start(bf16[1,144,256]{2,1,0:T(8,128)(2,1)} %get-tuple-element.116), channel_id=1, source_target_pairs={{0,16},{2,18},{4,20},{6,22},{8,24},{10,26},{12,28},{14,30},{16,0},... | collective-permute-start | bytes 221192 | tf_op jit(solution)/shard_map/ppermute | solution.py:176
  5.8 1.4 %collective-permute-start.3 = (bf16[1,144,256]{2,1,0:T(8,128)(2,1)}, bf16[1,144,256]{2,1,0:T(8,128)(2,1)S(1)}, u32[]{:S(2)}, u32[]{:S(2)}) collective-permute-start(bf16[1,144,256]{2,1,0:T(8,128)(2,1)} %get-tuple-element.117), channel_id=1, source_target_pairs={{0,24},{2,26},{4,28},{6,30},{8,0},{10,2},{12,4},{14,6},{16,8},{18,... | collective-permute-start | bytes 221192 | tf_op jit(solution)/shard_map/ppermute | solution.py:176
  7.1 0.0 copy-start.3
  7.1 0.0 copy-start.2
  7.1 0.0 copy-start.1
  7.1 4.7 %all-to-all-start.1 = ((bf16[16,2,128,256]{3,2,1,0:T(8,128)(2,1)}), bf16[16,2,128,256]{3,2,1,0:T(8,128)(2,1)S(1)}, u32[]{:S(2)}, u32[]{:S(2)}) async-start(bf16[16,2,128,256]{3,2,1,0:T(8,128)(2,1)} %bitcast.17), calls=%async_computation.1 | async-start | bytes 4194304 | tf_op jit(solution)/shard_map/all_to_all | solution.py:622
  11.9 0.0 copy-done.3
  11.9 0.1 reduce_sum.9
  12.0 0.1 divide_convert_fusion
  12.1 0.0 copy-done.2
  12.1 0.7 stack.44.shifts
  12.8 0.5 fusion.5.source
  13.3 0.0 collective-permute-done.1
  13.3 0.0 collective-permute-done.2
  13.3 0.0 collective-permute-done.3
  13.4 1.2 %collective-permute-start.4 = (bf16[4,144,256]{2,1,0:T(8,128)(2,1)S(1)}, bf16[4,144,256]{2,1,0:T(8,128)(2,1)}, u32[]{:S(2)}, u32[]{:S(2)}) collective-permute-start(bf16[4,144,256]{2,1,0:T(8,128)(2,1)S(1)} %constant_dynamic-update-slice_fusion.refs_0_), channel_id=1, source_target_pairs={{0,2},{2,0},{4,6},{6,4},{8,10},{10,8},{12,14},{14,12},{16,18},{18,... | collective-permute-start | bytes 884744 | tf_op jit(solution)/shard_map/ppermute | solution.py:187
  14.6 0.3 collective-permute-start.5
  14.9 1.2 %collective-permute-start.6 = (bf16[4,144,256]{2,1,0:T(8,128)(2,1)S(1)}, bf16[4,144,256]{2,1,0:T(8,128)(2,1)}, u32[]{:S(2)}, u32[]{:S(2)}) collective-permute-start(bf16[4,144,256]{2,1,0:T(8,128)(2,1)S(1)} %constant_dynamic-update-slice_fusion.refs_0_), channel_id=1, source_target_pairs={{0,6},{2,4},{4,2},{6,0},{8,14},{10,12},{12,10},{14,8},{16,22},{18,... | collective-permute-start | bytes 884744 | tf_op jit(solution)/shard_map/ppermute | solution.py:187
  16.1 0.1 rev.3
  16.2 0.0 copy-done.1
  16.2 3.0 %collective-permute-start.7 = (f32[4,64,256]{2,1,0:T(8,128)S(1)}, f32[4,64,256]{2,1,0:T(8,128)S(1)}, u32[]{:S(2)}, u32[]{:S(2)}) collective-permute-start(f32[4,64,256]{2,1,0:T(8,128)S(1)} %constant_dynamic-slice_fusion.2), channel_id=1, source_target_pairs={{0,1},{1,0},{2,3},{3,2},{4,5},{5,4},{6,7},{7,6},{8,9},{9,8},{10,11... | collective-permute-start | bytes 786440 | tf_op jit(solution)/shard_map/ppermute | solution.py:247
  19.2 0.6 fusion.3.taps_rows
  19.8 6.1 %bands.1 = (bf16[6,176,192]{2,1,0:T(8,128)(2,1)}, bf16[6,160,176]{2,1,0:T(8,128)(2,1)}, bf16[6,144,160]{2,1,0:T(8,128)(2,1)}, bf16[6,128,144]{2,1,0:T(8,128)(2,1)}) custom-call(s32[8]{0:T(128)} %stack.44.shifts, f32[2,6,256]{2,1,0:T(8,128)} %fusion.3.taps_rows), custom_call_target="tpu_custom_call" | custom-call | flops 99999997952 | tf_op jit(solution)/shard_map/bands/pallas_call | solution.py:335
  25.9 0.0 collective-permute-done.7
  25.9 1.3 %maximum_select_fusion = f32[4,192,256]{2,1,0:T(8,128)S(1)} fusion(f32[4,64,256]{2,1,0:T(8,128)S(1)} %collective-permute-done.7, f32[4,128,256]{2,1,0:T(8,128)} %param.7, pred[]{:T(512)S(6)} %eq.4), kind=kLoop, calls=%fused_computation.1 | loop fusion | flops 589824 | bytes 1572865 | tf_op jit(solution)/shard_map/jit(_where)/select_n | solution.py:261
  27.2 0.0 collective-permute-done.4.refs_1_
  27.2 10.8 %collective-permute-done.5.refs_2_ = bf16[4,144,256]{2,1,0:T(8,128)(2,1)} collective-permute-done((bf16[4,144,256]{2,1,0:T(8,128)(2,1)S(1)}, bf16[4,144,256]{2,1,0:T(8,128)(2,1)}, u32[]{:S(2)}, u32[]{:S(2)}) %collective-permute-start.5) | collective-permute-done | bytes 294944 | tf_op jit(solution)/shard_map/ppermute | solution.py:187
  38.0 0.0 collective-permute-done.6.refs_3_
  38.0 0.0 copy-start.4
  38.0 1.8 %ends.1 = bf16[16,48,256]{2,1,0:T(8,128)(2,1)} custom-call(s32[1]{0:T(128)} %bitcast.10.start, bf16[4,144,256]{2,1,0:T(8,128)(2,1)S(1)} %constant_dynamic-update-slice_fusion.refs_0_, bf16[4,144,256]{2,1,0:T(8,128)(2,1)} %collective-permute-done.4.refs_1_, bf16[4,144,256]{2,1,0:T(8,128)(2,1)} %collective-permute-done.5.refs_2_, ...), custom_call_target="tpu_custom_call" | custom-call | tf_op jit(solution)/shard_map/ends/pallas_call | solution.py:228
  39.8 4.2 %collective-permute-start.8 = (bf16[16,48,256]{2,1,0:T(8,128)(2,1)}, bf16[16,48,256]{2,1,0:T(8,128)(2,1)}, u32[]{:S(2)}, u32[]{:S(2)}) collective-permute-start(bf16[16,48,256]{2,1,0:T(8,128)(2,1)} %ends.1), channel_id=1, source_target_pairs={{0,1},{1,0},{2,3},{3,2},{4,5},{5,4},{6,7},{7,6},{8,9},{9,8},{10,11... | collective-permute-start | bytes 1179656 | tf_op jit(solution)/shard_map/ppermute | solution.py:247
  44.0 0.6 pad_add_fusion.place
  44.6 3.8 %plan.1 = (s32[199]{0:T(256)S(1)}, s32[1]{0:T(128)}) custom-call(s32[2]{0:T(128)} %pad_add_fusion.place, s32[16]{0:T(128)} %fusion.5.source, bf16[4,144,256]{2,1,0:T(8,128)(2,1)S(1)} %constant_dynamic-update-slice_fusion.refs_0_, bf16[4,144,256]{2,1,0:T(8,128)(2,1)} %collective-permute-done.4.refs_1_, bf16[4,144,256]{2,1,0:T(8,128)(2,1)} %collective-permute-done.5.refs_2_, ...), custom_call_target="tpu_custom_call" | custom-call | tf_op jit(solution)/shard_map/plan/pallas_call | solution.py:419
  48.4 0.0 collective-permute-done.8
  48.4 11.6 %all-to-all-done.1 = bf16[16,2,128,256]{3,2,1,0:T(8,128)(2,1)S(1)} async-done(((bf16[16,2,128,256]{3,2,1,0:T(8,128)(2,1)}), bf16[16,2,128,256]{3,2,1,0:T(8,128)(2,1)S(1)}, u32[]{:S(2)}, u32[]{:S(2)}) %all-to-all-start.1) | async-done | bytes 2097184 | tf_op jit(solution)/shard_map/all_to_all | solution.py:622
  60.0 0.1 constant_dynamic-slice_fusion.1
  60.1 1.5 %collective-permute-start.9 = (bf16[32,48,256]{2,1,0:T(8,128)(2,1)S(1)}, bf16[32,48,256]{2,1,0:T(8,128)(2,1)}, u32[]{:S(2)}, u32[]{:S(2)}) collective-permute-start(bf16[32,48,256]{2,1,0:T(8,128)(2,1)S(1)} %constant_dynamic-slice_fusion.1), channel_id=1, source_target_pairs={{0,1},{1,0},{2,3},{3,2},{4,5},{5,4},{6,7},{7,6},{8,9},{9,8},{10,11... | collective-permute-start | bytes 2359304 | tf_op jit(solution)/shard_map/ppermute | solution.py:247
  62.3 1.3 %collective-permute-done.9 = bf16[32,48,256]{2,1,0:T(8,128)(2,1)} collective-permute-done((bf16[32,48,256]{2,1,0:T(8,128)(2,1)S(1)}, bf16[32,48,256]{2,1,0:T(8,128)(2,1)}, u32[]{:S(2)}, u32[]{:S(2)}) %collective-permute-start.9) | collective-permute-done | bytes 786464 | tf_op jit(solution)/shard_map/ppermute | solution.py:247
  63.6 0.0 copy-done.4
  63.6 6.0 %conditional.1 = (f32[4,128,256]{2,1,0:T(8,128)}) conditional(s32[]{:T(128)} %bitcast.13, (s32[199]{0:T(256)S(1)}, bf16[32,128,256]{2,1,0:T(8,128)(2,1)S(1)}, f32[4,192,256]{2,1,0:T(8,128)S(1)}, bf16[4,144,256]{2,1,0:T(8,128)(2,1)S(1)}, bf16[4,144,256]{2,1,0:T(8,128)(2,1)}, /*index=5*/bf16[4,144,256]{2,1,0:T(8,128)(2,1)}, ...), branch_computations={%region_1.2_spmd, %region_2.3_spmd} | conditional | flops 4 | bytes 8650906 | solution.py:663
  63.6 6.0 %deconvolve.2 = f32[4,128,256]{2,1,0:T(8,128)} custom-call(s32[199]{0:T(256)S(1)} %get-tuple-element.54.lists, bf16[32,128,256]{2,1,0:T(8,128)(2,1)S(1)} %get-tuple-element.55.main, f32[4,192,256]{2,1,0:T(8,128)S(1)} %get-tuple-element.56.est, bf16[4,144,256]{2,1,0:T(8,128)(2,1)S(1)} %get-tuple-element.57.refs_0_, ...), custom_call_target="tpu_custom_call" | custom-call | tf_op jit(solution)/shard_map/cond/branch_0_fun/deconvolve/pallas_call | solution.py:588
  (5 shorter events, 0.0 us)
Async XLA Ops:
  3.3 10.0 %collective-permute-start.1 = (bf16[1,144,256]{2,1,0:T(8,128)(2,1)}, bf16[1,144,256]{2,1,0:T(8,128)(2,1)S(1)}, u32[]{:S(2)}, u32[]{:S(2)}) collective-permute-start(bf16[1,144,256]{2,1,0:T(8,128)(2,1)} %get-tuple-element.115), channel_id=1, source_target_pairs={{0,8},{2,10},{4,12},{6,14},{8,16},{10,18},{12,20},{14,22},{16,24},... | collective-permute-start | bytes 221192 | tf_op jit(solution)/shard_map/ppermute | solution.py:176
  4.6 8.7 %collective-permute-start.2 = (bf16[1,144,256]{2,1,0:T(8,128)(2,1)}, bf16[1,144,256]{2,1,0:T(8,128)(2,1)S(1)}, u32[]{:S(2)}, u32[]{:S(2)}) collective-permute-start(bf16[1,144,256]{2,1,0:T(8,128)(2,1)} %get-tuple-element.116), channel_id=1, source_target_pairs={{0,16},{2,18},{4,20},{6,22},{8,24},{10,26},{12,28},{14,30},{16,0},... | collective-permute-start | bytes 221192 | tf_op jit(solution)/shard_map/ppermute | solution.py:176
  5.8 7.6 %collective-permute-start.3 = (bf16[1,144,256]{2,1,0:T(8,128)(2,1)}, bf16[1,144,256]{2,1,0:T(8,128)(2,1)S(1)}, u32[]{:S(2)}, u32[]{:S(2)}) collective-permute-start(bf16[1,144,256]{2,1,0:T(8,128)(2,1)} %get-tuple-element.117), channel_id=1, source_target_pairs={{0,24},{2,26},{4,28},{6,30},{8,0},{10,2},{12,4},{14,6},{16,8},{18,... | collective-permute-start | bytes 221192 | tf_op jit(solution)/shard_map/ppermute | solution.py:176
  7.1 4.7 %copy-start.3 = (f32[6,33]{1,0:T(8,128)S(1)}, f32[6,33]{1,0:T(8,128)}, u32[]{:S(2)}) copy-start(f32[6,33]{1,0:T(8,128)} %param.11) | copy-start | bytes 2380
  7.1 4.9 %copy-start.2 = (bf16[1,144,256]{2,1,0:T(8,128)(2,1)S(1)}, bf16[1,144,256]{2,1,0:T(8,128)(2,1)}, u32[]{:S(2)}) copy-start(bf16[1,144,256]{2,1,0:T(8,128)(2,1)} %get-tuple-element.114) | copy-start | bytes 221188
  7.1 9.0 %copy-start.1 = (f32[4,128,256]{2,1,0:T(8,128)S(1)}, f32[4,128,256]{2,1,0:T(8,128)}, u32[]{:S(2)}) copy-start(f32[4,128,256]{2,1,0:T(8,128)} %param.7) | copy-start | bytes 1572868
  7.1 52.9 %all-to-all-start.1 = ((bf16[16,2,128,256]{3,2,1,0:T(8,128)(2,1)}), bf16[16,2,128,256]{3,2,1,0:T(8,128)(2,1)S(1)}, u32[]{:S(2)}, u32[]{:S(2)}) async-start(bf16[16,2,128,256]{3,2,1,0:T(8,128)(2,1)} %bitcast.17), calls=%async_computation.1 | async-start | bytes 4194304 | tf_op jit(solution)/shard_map/all_to_all | solution.py:622
  13.4 13.8 %collective-permute-start.4 = (bf16[4,144,256]{2,1,0:T(8,128)(2,1)S(1)}, bf16[4,144,256]{2,1,0:T(8,128)(2,1)}, u32[]{:S(2)}, u32[]{:S(2)}) collective-permute-start(bf16[4,144,256]{2,1,0:T(8,128)(2,1)S(1)} %constant_dynamic-update-slice_fusion.refs_0_), channel_id=1, source_target_pairs={{0,2},{2,0},{4,6},{6,4},{8,10},{10,8},{12,14},{14,12},{16,18},{18,... | collective-permute-start | bytes 884744 | tf_op jit(solution)/shard_map/ppermute | solution.py:187
  14.6 23.4 %collective-permute-start.5 = (bf16[4,144,256]{2,1,0:T(8,128)(2,1)S(1)}, bf16[4,144,256]{2,1,0:T(8,128)(2,1)}, u32[]{:S(2)}, u32[]{:S(2)}) collective-permute-start(bf16[4,144,256]{2,1,0:T(8,128)(2,1)S(1)} %constant_dynamic-update-slice_fusion.refs_0_), channel_id=1, source_target_pairs={{0,4},{2,6},{4,0},{6,2},{8,12},{10,14},{12,8},{14,10},{16,20},{18,... | collective-permute-start | bytes 884744 | tf_op jit(solution)/shard_map/ppermute | solution.py:187
  14.9 23.1 %collective-permute-start.6 = (bf16[4,144,256]{2,1,0:T(8,128)(2,1)S(1)}, bf16[4,144,256]{2,1,0:T(8,128)(2,1)}, u32[]{:S(2)}, u32[]{:S(2)}) collective-permute-start(bf16[4,144,256]{2,1,0:T(8,128)(2,1)S(1)} %constant_dynamic-update-slice_fusion.refs_0_), channel_id=1, source_target_pairs={{0,6},{2,4},{4,2},{6,0},{8,14},{10,12},{12,10},{14,8},{16,22},{18,... | collective-permute-start | bytes 884744 | tf_op jit(solution)/shard_map/ppermute | solution.py:187
  16.2 9.7 %collective-permute-start.7 = (f32[4,64,256]{2,1,0:T(8,128)S(1)}, f32[4,64,256]{2,1,0:T(8,128)S(1)}, u32[]{:S(2)}, u32[]{:S(2)}) collective-permute-start(f32[4,64,256]{2,1,0:T(8,128)S(1)} %constant_dynamic-slice_fusion.2), channel_id=1, source_target_pairs={{0,1},{1,0},{2,3},{3,2},{4,5},{5,4},{6,7},{7,6},{8,9},{9,8},{10,11... | collective-permute-start | bytes 786440 | tf_op jit(solution)/shard_map/ppermute | solution.py:247
  38.0 25.6 %copy-start.4 = (s32[4,6]{1,0:T(4,128)S(1)}, s32[4,6]{1,0:T(4,128)}, u32[]{:S(2)}) copy-start(s32[4,6]{1,0:T(4,128)} %owners.1) | copy-start | bytes 292
  39.8 8.7 %collective-permute-start.8 = (bf16[16,48,256]{2,1,0:T(8,128)(2,1)}, bf16[16,48,256]{2,1,0:T(8,128)(2,1)}, u32[]{:S(2)}, u32[]{:S(2)}) collective-permute-start(bf16[16,48,256]{2,1,0:T(8,128)(2,1)} %ends.1), channel_id=1, source_target_pairs={{0,1},{1,0},{2,3},{3,2},{4,5},{5,4},{6,7},{7,6},{8,9},{9,8},{10,11... | collective-permute-start | bytes 1179656 | tf_op jit(solution)/shard_map/ppermute | solution.py:247
  60.1 3.6 %collective-permute-start.9 = (bf16[32,48,256]{2,1,0:T(8,128)(2,1)S(1)}, bf16[32,48,256]{2,1,0:T(8,128)(2,1)}, u32[]{:S(2)}, u32[]{:S(2)}) collective-permute-start(bf16[32,48,256]{2,1,0:T(8,128)(2,1)S(1)} %constant_dynamic-slice_fusion.1), channel_id=1, source_target_pairs={{0,1},{1,0},{2,3},{3,2},{4,5},{5,4},{6,7},{7,6},{8,9},{9,8},{10,11... | collective-permute-start | bytes 2359304 | tf_op jit(solution)/shard_map/ppermute | solution.py:247
where the time goes:
time: 70.8 us; the launch traced here: 69.7 us
  waiting for transfers between devices  23.7 us (33%)
  Pallas kernels  21 us (30%)
  starting transfers between devices  20 us (28%)
  other arithmetic  3.21 us (5%)
  local copies, waits for them, and re-layouts  0.89 us (1%)
  between operations  0.82 us (1%)
    all_to_all x1, waiting for transfers between devices, local(): lax.all_to_all(packed.reshape(peers, MAIN, depth, lat), 'join', split_axi...  11.6 us
    ppermute x3, waiting for transfers between devices, among_members(): parts.append(lax.ppermute(line, 'join', [(i, i ^ m) for i in range(peers)]))  10.8 us
    ppermute x3, starting transfers between devices, halos(): return [lax.ppermute(sent, 'view', [(0, 1), (1, 0)])]  8.75 us
    pallas_call x1, Pallas kernels, bands(): pl.pallas_call(functools.partial(bands_kernel, shapes), out_shape=outs, i...  6.11 us
    pallas_call x1, Pallas kernels, deconvolve(): pl.pallas_call(functools.partial(deconvolve_kernel, starts, len(parts), s...  6.01 us
    all_to_all x1, starting transfers between devices, local(): lax.all_to_all(packed.reshape(peers, MAIN, depth, lat), 'join', split_axi...  4.72 us
    ppermute x3, starting transfers between devices, along_groups(): lax.ppermute(rows[k], 'join', [(i, (i + k * members) % peers) for i in ra...  3.83 us
    pallas_call x1, Pallas kernels, plan(): pl.pallas_call(functools.partial(plan_kernel, nviews, blocks), out_shape=...  3.81 us
  transfers between devices with their start and end apart: 10, of which 3 were waited for; matrix products, arithmetic and copies ran while one was open for 6% of the time, Pallas kernels for 17%

commit v1 on v0

--- a/solution.py
+++ b/solution.py
@@ -434,27 +434,31 @@
     )(jnp.stack([here, low_rows()]), source, *parts)
 
 
-def deconvolve_kernel(starts, nparts, sides, guard, lists, main, est, *refs):
+def deconvolve_kernel(starts, nparts, sides, guard, listed, main, est, *refs):
     main_slot, main_code, third_slot, third_code, numbers = starts
     parts, third_halo, refs = refs[:nparts], refs[nparts : nparts + sides], refs[nparts + sides :]
     number = 2 * ITERS + sides
     sources, out, refs = refs[:number], refs[number], refs[number + 1 :]
     copied, refs = refs[:number], refs[number:]
     bands_of, main_halo = copied[: 2 * ITERS], copied[2 * ITERS :]
-    held, recip, following, total, result, own_sems, held_sems, out_sems = refs
+    lists, held, recip, following, total, result, own_sems, held_sems, out_sems, lists_sem = refs
     blocks, depth, lat = out.shape
     nviews = bands_of[0].shape[0]
     per_part = parts[0].shape[0]
-    mains, thirds = lists[numbers], lists[numbers + 1]
-    low = pl.multiple_of(lists[numbers + 2], H)
-    counts = [lists[numbers + 3 + b] for b in range(blocks)]
     own = [
         pltpu.make_async_copy(source, to, own_sems.at[k])
         for k, (source, to) in enumerate(zip(sources, copied))
     ]
-    for copy in own:
+    own[0].start()
+    listing = pltpu.make_async_copy(listed, lists, lists_sem)
+    listing.start()
+    for copy in own[1:]:
         copy.start()
-
+    listing.wait()
+
+    mains, thirds = lists[numbers], lists[numbers + 1]
+    low = pl.multiple_of(lists[numbers + 2], H)
+    counts = [lists[numbers + 3 + b] for b in range(blocks)]
     def copies(p, part, at, slot):
         yield pltpu.make_async_copy(
             part.at[at, pl.ds(0, depth)], held.at[p, pl.ds(0, depth)], held_sems.at[p, 0]
@@ -488,16 +492,13 @@
         halo_at = [pl.multiple_of(2 * sweep * low, 2 * H), 0]
         own[2 * sweep].wait()
         for b in range(blocks):
-
-            @pl.when(counts[b] > 0)
-            def _():
-                rounded = current[b, : forward.shape[2]].astype(jnp.bfloat16)
-                for v in range(nviews):
-                    blurred = jnp.dot(forward[v], rounded, preferred_element_type=jnp.float32)
-                    inverse = 1.0 / blurred
-                    if guard:
-                        inverse = jnp.where(blurred > 0, inverse, 0.0)
-                    recip[b * nviews + v, :view_rows] = inverse
+            rounded = current[b, : forward.shape[2]].astype(jnp.bfloat16)
+            for v in range(nviews):
+                blurred = jnp.dot(forward[v], rounded, preferred_element_type=jnp.float32)
+                inverse = 1.0 / blurred
+                if guard:
+                    inverse = jnp.where(blurred > 0, inverse, 0.0)
+                recip[b * nviews + v, :view_rows] = inverse
 
         total[:, :next_rows] = jnp.zeros((blocks + 1, next_rows, lat), jnp.float32)
 
@@ -552,24 +553,13 @@
 
         add(thirds, third_rows, third_code)
         for b in range(blocks):
-
-            @pl.when(counts[b] > 0)
-            def _():
-                updated = current[b, pl.ds(next_at, next_rows)] * (
-                    total[b, :next_rows] / counts[b].astype(jnp.float32)
-                )
-                if sweep < ITERS - 1:
-                    following[b, :next_rows] = updated
-                else:
-                    result[b] = updated
-
-            if sweep == ITERS - 1:
-
-                @pl.when(counts[b] == 0)
-                def _():
-                    at = pl.multiple_of(2 * ITERS * low, 2 * H)
-                    result[b] = est[b, pl.ds(at, depth)]
-
+            average = total[b, :next_rows] / jnp.maximum(counts[b], 1).astype(jnp.float32)
+            factor = jnp.where(counts[b] > 0, average, 1.0)
+            updated = current[b, pl.ds(next_at, next_rows)] * factor
+            if sweep < ITERS - 1:
+                following[b, :next_rows] = updated
+            else:
+                result[b] = updated
                 store = pltpu.make_async_copy(result.at[b], out.at[b], out_sems.at[b])
                 store.start()
                 stores.append(store)
@@ -588,10 +578,11 @@
     return pl.pallas_call(
         functools.partial(deconvolve_kernel, starts, len(parts), sides, guard),
         out_shape=pltpu.HBM((blocks, depth, lat), jnp.float32),
-        in_specs=[SMEM] + [VMEM] * 2 + [ANY] * len(in_place),
+        in_specs=[ANY] + [VMEM] * 2 + [ANY] * len(in_place),
         out_specs=HBM,
         scratch_shapes=[pltpu.VMEM(array.shape, array.dtype) for array in copied]
         + [
+            pltpu.SMEM(lists.shape, lists.dtype),
             pltpu.VMEM((thirds, view_rows, lat), jnp.bfloat16),
             pltpu.VMEM((blocks * nviews + 1, view_rows, lat), jnp.float32),
             pltpu.VMEM((blocks, *following), jnp.float32),
@@ -600,6 +591,7 @@
             pltpu.SemaphoreType.DMA((len(copied),)),
             pltpu.SemaphoreType.DMA((thirds, 1 + sides)),
             pltpu.SemaphoreType.DMA((blocks,)),
+            pltpu.SemaphoreType.DMA,
         ],
         compiler_params=pltpu.CompilerParams(vmem_limit_bytes=24 * 1024 * 1024),
         name="deconvolve",

time: 70.8 us -> 70.3 us (level)
  the two profiles are of different devices: /device:TPU:13 before, /device:TPU:17 now
where the time goes in v1:
time: 70.3 us; the launch traced here: 68.9 us
  waiting for transfers between devices  23.9 us (34%)
  Pallas kernels  21 us (30%)
  starting transfers between devices  19 us (27%)
  other arithmetic  3.21 us (5%)
  local copies, waits for them, and re-layouts  0.89 us (1%)
  between operations  0.82 us (1%)
    ppermute x3, waiting for transfers between devices, among_members(): parts.append(lax.ppermute(line, 'join', [(i, i ^ m) for i in range(peers)]))  14.1 us
    all_to_all x1, waiting for transfers between devices, local(): lax.all_to_all(packed.reshape(peers, MAIN, depth, lat), 'join', split_axi...  8.44 us
    ppermute x3, starting transfers between devices, halos(): return [lax.ppermute(sent, 'view', [(0, 1), (1, 0)])]  7.85 us
    pallas_call x1, Pallas kernels, bands(): pl.pallas_call(functools.partial(bands_kernel, shapes), out_shape=outs, i...  6.11 us
    pallas_call x1, Pallas kernels, deconvolve(): pl.pallas_call(functools.partial(deconvolve_kernel, starts, len(parts), s...  6.06 us
    all_to_all x1, starting transfers between devices, local(): lax.all_to_all(packed.reshape(peers, MAIN, depth, lat), 'join', split_axi...  5.91 us
    pallas_call x1, Pallas kernels, plan(): pl.pallas_call(functools.partial(plan_kernel, nviews, blocks), out_shape=...  3.81 us
    pallas_call x1, Pallas kernels, pack(): pl.pallas_call(pack_kernel, out_shape=(jax.ShapeDtypeStruct((peers * MAIN...  3.29 us
  transfers between devices with their start and end apart: 10, of which 3 were waited for; matrix products, arithmetic and copies ran while one was open for 6% of the time, Pallas kernels for 17%

profile of v1, /device:TPU:17, one launch (start us, length us, event | category | flops | bytes accessed | tf_op | source)
XLA Modules:
  0.0 68.9 jit_solution(8226485473969443265)
XLA Ops:
  0.0 3.3 %pack.1 = (bf16[32,128,256]{2,1,0:T(8,128)(2,1)}, bf16[1,144,256]{2,1,0:T(8,128)(2,1)}, bf16[1,144,256]{2,1,0:T(8,128)(2,1)}, bf16[1,144,256]{2,1,0:T(8,128)(2,1)}, bf16[1,144,256]{2,1,0:T(8,128)(2,1)}) custom-call(s32[4,6]{1,0:T(4,128)} %owners.1, s32[4,6]{1,0:T(4,128)} %blocks_of.1, s32[1]{0:T(128)} %bitcast.here, bf16[4,6,128,256]{3,2,1,0:T(8,128)(2,1)} %views.1), custom_call_target="tpu_custom_call" | custom-call | tf_op jit(solution)/shard_map/pack/pallas_call | solution.py:104
  3.3 1.3 %collective-permute-start.1 = (bf16[1,144,256]{2,1,0:T(8,128)(2,1)}, bf16[1,144,256]{2,1,0:T(8,128)(2,1)S(1)}, u32[]{:S(2)}, u32[]{:S(2)}) collective-permute-start(bf16[1,144,256]{2,1,0:T(8,128)(2,1)} %get-tuple-element.115), channel_id=1, source_target_pairs={{0,8},{2,10},{4,12},{6,14},{8,16},{10,18},{12,20},{14,22},{16,24},... | collective-permute-start | bytes 221192 | tf_op jit(solution)/shard_map/ppermute | solution.py:176
  4.6 0.1 collective-permute-start.2
  4.7 1.1 %collective-permute-start.3 = (bf16[1,144,256]{2,1,0:T(8,128)(2,1)}, bf16[1,144,256]{2,1,0:T(8,128)(2,1)S(1)}, u32[]{:S(2)}, u32[]{:S(2)}) collective-permute-start(bf16[1,144,256]{2,1,0:T(8,128)(2,1)} %get-tuple-element.117), channel_id=1, source_target_pairs={{0,24},{2,26},{4,28},{6,30},{8,0},{10,2},{12,4},{14,6},{16,8},{18,... | collective-permute-start | bytes 221192 | tf_op jit(solution)/shard_map/ppermute | solution.py:176
  5.9 0.0 copy-start.3
  5.9 0.0 copy-start.2
  5.9 0.0 copy-start.1
  5.9 5.9 %all-to-all-start.1 = ((bf16[16,2,128,256]{3,2,1,0:T(8,128)(2,1)}), bf16[16,2,128,256]{3,2,1,0:T(8,128)(2,1)S(1)}, u32[]{:S(2)}, u32[]{:S(2)}) async-start(bf16[16,2,128,256]{3,2,1,0:T(8,128)(2,1)} %bitcast.17), calls=%async_computation.1 | async-start | bytes 4194304 | tf_op jit(solution)/shard_map/all_to_all | solution.py:614
  11.8 0.0 copy-done.3
  11.8 0.1 reduce_sum.9
  11.9 0.1 divide_convert_fusion
  12.0 0.0 copy-done.2
  12.0 0.7 %stack.44.shifts = s32[8]{0:T(128)} concatenate(s32[1]{0:T(128)} %bitcast.3, s32[1]{0:T(128)} %bitcast.4, s32[1]{0:T(128)} %bitcast.5, s32[1]{0:T(128)} %bitcast.6, s32[1]{0:T(128)} %bitcast.7, s32[1]{0:T(128)} %constant.102.clone.1, s32[1]{0:T(128)} %bitcast.5, s32[1]{0:T(128)} %bitcast.6), dimensions={0} | concatenate | bytes 64 | tf_op jit(solution)/shard_map/stack | solution.py:342
  12.7 0.5 fusion.5.source
  13.2 0.0 collective-permute-done.1
  13.2 0.0 collective-permute-done.2
  13.3 0.0 collective-permute-done.3
  13.3 1.3 %collective-permute-start.4 = (bf16[4,144,256]{2,1,0:T(8,128)(2,1)S(1)}, bf16[4,144,256]{2,1,0:T(8,128)(2,1)}, u32[]{:S(2)}, u32[]{:S(2)}) collective-permute-start(bf16[4,144,256]{2,1,0:T(8,128)(2,1)S(1)} %constant_dynamic-update-slice_fusion.refs_0_), channel_id=1, source_target_pairs={{0,2},{2,0},{4,6},{6,4},{8,10},{10,8},{12,14},{14,12},{16,18},{18,... | collective-permute-start | bytes 884744 | tf_op jit(solution)/shard_map/ppermute | solution.py:187
  14.5 1.2 %collective-permute-start.5 = (bf16[4,144,256]{2,1,0:T(8,128)(2,1)S(1)}, bf16[4,144,256]{2,1,0:T(8,128)(2,1)}, u32[]{:S(2)}, u32[]{:S(2)}) collective-permute-start(bf16[4,144,256]{2,1,0:T(8,128)(2,1)S(1)} %constant_dynamic-update-slice_fusion.refs_0_), channel_id=1, source_target_pairs={{0,4},{2,6},{4,0},{6,2},{8,12},{10,14},{12,8},{14,10},{16,20},{18,... | collective-permute-start | bytes 884744 | tf_op jit(solution)/shard_map/ppermute | solution.py:187
  15.7 0.3 collective-permute-start.6
  16.0 0.1 rev.3
  16.1 0.0 copy-done.1
  16.1 2.9 %collective-permute-start.7 = (f32[4,64,256]{2,1,0:T(8,128)S(1)}, f32[4,64,256]{2,1,0:T(8,128)S(1)}, u32[]{:S(2)}, u32[]{:S(2)}) collective-permute-start(f32[4,64,256]{2,1,0:T(8,128)S(1)} %constant_dynamic-slice_fusion.2), channel_id=1, source_target_pairs={{0,1},{1,0},{2,3},{3,2},{4,5},{5,4},{6,7},{7,6},{8,9},{9,8},{10,11... | collective-permute-start | bytes 786440 | tf_op jit(solution)/shard_map/ppermute | solution.py:247
  19.0 0.6 fusion.3.taps_rows
  19.6 6.1 %bands.1 = (bf16[6,176,192]{2,1,0:T(8,128)(2,1)}, bf16[6,160,176]{2,1,0:T(8,128)(2,1)}, bf16[6,144,160]{2,1,0:T(8,128)(2,1)}, bf16[6,128,144]{2,1,0:T(8,128)(2,1)}) custom-call(s32[8]{0:T(128)} %stack.44.shifts, f32[2,6,256]{2,1,0:T(8,128)} %fusion.3.taps_rows), custom_call_target="tpu_custom_call" | custom-call | flops 99999997952 | tf_op jit(solution)/shard_map/bands/pallas_call | solution.py:335
  25.8 0.0 collective-permute-done.7
  25.8 1.3 %maximum_select_fusion = f32[4,192,256]{2,1,0:T(8,128)S(1)} fusion(f32[4,64,256]{2,1,0:T(8,128)S(1)} %collective-permute-done.7, f32[4,128,256]{2,1,0:T(8,128)} %param.7, pred[]{:T(512)S(6)} %eq.4), kind=kLoop, calls=%fused_computation.1 | loop fusion | flops 589824 | bytes 1572865 | tf_op jit(solution)/shard_map/jit(_where)/select_n | solution.py:261
  27.1 0.0 collective-permute-done.4.refs_1_
  27.1 14.1 %collective-permute-done.5.refs_2_ = bf16[4,144,256]{2,1,0:T(8,128)(2,1)} collective-permute-done((bf16[4,144,256]{2,1,0:T(8,128)(2,1)S(1)}, bf16[4,144,256]{2,1,0:T(8,128)(2,1)}, u32[]{:S(2)}, u32[]{:S(2)}) %collective-permute-start.5) | collective-permute-done | bytes 294944 | tf_op jit(solution)/shard_map/ppermute | solution.py:187
  41.2 0.0 collective-permute-done.6.refs_3_
  41.2 0.0 copy-start.4
  41.2 1.8 %ends.1 = bf16[16,48,256]{2,1,0:T(8,128)(2,1)} custom-call(s32[1]{0:T(128)} %bitcast.10.start, bf16[4,144,256]{2,1,0:T(8,128)(2,1)S(1)} %constant_dynamic-update-slice_fusion.refs_0_, bf16[4,144,256]{2,1,0:T(8,128)(2,1)} %collective-permute-done.4.refs_1_, bf16[4,144,256]{2,1,0:T(8,128)(2,1)} %collective-permute-done.5.refs_2_, ...), custom_call_target="tpu_custom_call" | custom-call | tf_op jit(solution)/shard_map/ends/pallas_call | solution.py:228
  43.0 2.6 %collective-permute-start.8 = (bf16[16,48,256]{2,1,0:T(8,128)(2,1)}, bf16[16,48,256]{2,1,0:T(8,128)(2,1)}, u32[]{:S(2)}, u32[]{:S(2)}) collective-permute-start(bf16[16,48,256]{2,1,0:T(8,128)(2,1)} %ends.1), channel_id=1, source_target_pairs={{0,1},{1,0},{2,3},{3,2},{4,5},{5,4},{6,7},{7,6},{8,9},{9,8},{10,11... | collective-permute-start | bytes 1179656 | tf_op jit(solution)/shard_map/ppermute | solution.py:247
  45.6 0.6 pad_add_fusion.place
  46.2 3.8 %plan.1 = (s32[199]{0:T(256)S(1)}, s32[1]{0:T(128)}) custom-call(s32[2]{0:T(128)} %pad_add_fusion.place, s32[16]{0:T(128)} %fusion.5.source, bf16[4,144,256]{2,1,0:T(8,128)(2,1)S(1)} %constant_dynamic-update-slice_fusion.refs_0_, bf16[4,144,256]{2,1,0:T(8,128)(2,1)} %collective-permute-done.4.refs_1_, bf16[4,144,256]{2,1,0:T(8,128)(2,1)} %collective-permute-done.5.refs_2_, ...), custom_call_target="tpu_custom_call" | custom-call | tf_op jit(solution)/shard_map/plan/pallas_call | solution.py:419
  50.0 0.0 collective-permute-done.8
  50.0 8.4 %all-to-all-done.1 = bf16[16,2,128,256]{3,2,1,0:T(8,128)(2,1)S(1)} async-done(((bf16[16,2,128,256]{3,2,1,0:T(8,128)(2,1)}), bf16[16,2,128,256]{3,2,1,0:T(8,128)(2,1)S(1)}, u32[]{:S(2)}, u32[]{:S(2)}) %all-to-all-start.1) | async-done | bytes 2097184 | tf_op jit(solution)/shard_map/all_to_all | solution.py:614
  58.4 0.1 constant_dynamic-slice_fusion.1
  58.5 2.3 %collective-permute-start.9 = (bf16[32,48,256]{2,1,0:T(8,128)(2,1)S(1)}, bf16[32,48,256]{2,1,0:T(8,128)(2,1)}, u32[]{:S(2)}, u32[]{:S(2)}) collective-permute-start(bf16[32,48,256]{2,1,0:T(8,128)(2,1)S(1)} %constant_dynamic-slice_fusion.1), channel_id=1, source_target_pairs={{0,1},{1,0},{2,3},{3,2},{4,5},{5,4},{6,7},{7,6},{8,9},{9,8},{10,11... | collective-permute-start | bytes 2359304 | tf_op jit(solution)/shard_map/ppermute | solution.py:247
  61.5 1.3 %collective-permute-done.9 = bf16[32,48,256]{2,1,0:T(8,128)(2,1)} collective-permute-done((bf16[32,48,256]{2,1,0:T(8,128)(2,1)S(1)}, bf16[32,48,256]{2,1,0:T(8,128)(2,1)}, u32[]{:S(2)}, u32[]{:S(2)}) %collective-permute-start.9) | collective-permute-done | bytes 786464 | tf_op jit(solution)/shard_map/ppermute | solution.py:247
  62.8 0.0 copy-done.4
  62.8 6.1 %conditional.1 = (f32[4,128,256]{2,1,0:T(8,128)}) conditional(s32[]{:T(128)} %bitcast.13, (s32[199]{0:T(256)S(1)}, bf16[32,128,256]{2,1,0:T(8,128)(2,1)S(1)}, f32[4,192,256]{2,1,0:T(8,128)S(1)}, bf16[4,144,256]{2,1,0:T(8,128)(2,1)S(1)}, bf16[4,144,256]{2,1,0:T(8,128)(2,1)}, /*index=5*/bf16[4,144,256]{2,1,0:T(8,128)(2,1)}, ...), branch_computations={%region_1.2_spmd, %region_2.3_spmd} | conditional | flops 4 | bytes 8650906 | solution.py:655
  62.8 6.1 %deconvolve.2 = f32[4,128,256]{2,1,0:T(8,128)} custom-call(s32[199]{0:T(256)S(1)} %get-tuple-element.54.listed, bf16[32,128,256]{2,1,0:T(8,128)(2,1)S(1)} %get-tuple-element.55.main, f32[4,192,256]{2,1,0:T(8,128)S(1)} %get-tuple-element.56.est, bf16[4,144,256]{2,1,0:T(8,128)(2,1)S(1)} %get-tuple-element.57.refs_0_, ...), custom_call_target="tpu_custom_call" | custom-call | tf_op jit(solution)/shard_map/cond/branch_0_fun/deconvolve/pallas_call | solution.py:578
  (5 shorter events, 0.0 us)
Async XLA Ops:
  3.3 9.9 %collective-permute-start.1 = (bf16[1,144,256]{2,1,0:T(8,128)(2,1)}, bf16[1,144,256]{2,1,0:T(8,128)(2,1)S(1)}, u32[]{:S(2)}, u32[]{:S(2)}) collective-permute-start(bf16[1,144,256]{2,1,0:T(8,128)(2,1)} %get-tuple-element.115), channel_id=1, source_target_pairs={{0,8},{2,10},{4,12},{6,14},{8,16},{10,18},{12,20},{14,22},{16,24},... | collective-permute-start | bytes 221192 | tf_op jit(solution)/shard_map/ppermute | solution.py:176
  4.6 8.6 %collective-permute-start.2 = (bf16[1,144,256]{2,1,0:T(8,128)(2,1)}, bf16[1,144,256]{2,1,0:T(8,128)(2,1)S(1)}, u32[]{:S(2)}, u32[]{:S(2)}) collective-permute-start(bf16[1,144,256]{2,1,0:T(8,128)(2,1)} %get-tuple-element.116), channel_id=1, source_target_pairs={{0,16},{2,18},{4,20},{6,22},{8,24},{10,26},{12,28},{14,30},{16,0},... | collective-permute-start | bytes 221192 | tf_op jit(solution)/shard_map/ppermute | solution.py:176
  4.7 8.5 %collective-permute-start.3 = (bf16[1,144,256]{2,1,0:T(8,128)(2,1)}, bf16[1,144,256]{2,1,0:T(8,128)(2,1)S(1)}, u32[]{:S(2)}, u32[]{:S(2)}) collective-permute-start(bf16[1,144,256]{2,1,0:T(8,128)(2,1)} %get-tuple-element.117), channel_id=1, source_target_pairs={{0,24},{2,26},{4,28},{6,30},{8,0},{10,2},{12,4},{14,6},{16,8},{18,... | collective-permute-start | bytes 221192 | tf_op jit(solution)/shard_map/ppermute | solution.py:176
  5.9 5.9 %copy-start.3 = (f32[6,33]{1,0:T(8,128)S(1)}, f32[6,33]{1,0:T(8,128)}, u32[]{:S(2)}) copy-start(f32[6,33]{1,0:T(8,128)} %param.11) | copy-start | bytes 2380
  5.9 6.1 %copy-start.2 = (bf16[1,144,256]{2,1,0:T(8,128)(2,1)S(1)}, bf16[1,144,256]{2,1,0:T(8,128)(2,1)}, u32[]{:S(2)}) copy-start(bf16[1,144,256]{2,1,0:T(8,128)(2,1)} %get-tuple-element.114) | copy-start | bytes 221188
  5.9 10.2 %copy-start.1 = (f32[4,128,256]{2,1,0:T(8,128)S(1)}, f32[4,128,256]{2,1,0:T(8,128)}, u32[]{:S(2)}) copy-start(f32[4,128,256]{2,1,0:T(8,128)} %param.7) | copy-start | bytes 1572868
  5.9 52.6 %all-to-all-start.1 = ((bf16[16,2,128,256]{3,2,1,0:T(8,128)(2,1)}), bf16[16,2,128,256]{3,2,1,0:T(8,128)(2,1)S(1)}, u32[]{:S(2)}, u32[]{:S(2)}) async-start(bf16[16,2,128,256]{3,2,1,0:T(8,128)(2,1)} %bitcast.17), calls=%async_computation.1 | async-start | bytes 4194304 | tf_op jit(solution)/shard_map/all_to_all | solution.py:614
  13.3 13.8 %collective-permute-start.4 = (bf16[4,144,256]{2,1,0:T(8,128)(2,1)S(1)}, bf16[4,144,256]{2,1,0:T(8,128)(2,1)}, u32[]{:S(2)}, u32[]{:S(2)}) collective-permute-start(bf16[4,144,256]{2,1,0:T(8,128)(2,1)S(1)} %constant_dynamic-update-slice_fusion.refs_0_), channel_id=1, source_target_pairs={{0,2},{2,0},{4,6},{6,4},{8,10},{10,8},{12,14},{14,12},{16,18},{18,... | collective-permute-start | bytes 884744 | tf_op jit(solution)/shard_map/ppermute | solution.py:187
  14.5 26.7 %collective-permute-start.5 = (bf16[4,144,256]{2,1,0:T(8,128)(2,1)S(1)}, bf16[4,144,256]{2,1,0:T(8,128)(2,1)}, u32[]{:S(2)}, u32[]{:S(2)}) collective-permute-start(bf16[4,144,256]{2,1,0:T(8,128)(2,1)S(1)} %constant_dynamic-update-slice_fusion.refs_0_), channel_id=1, source_target_pairs={{0,4},{2,6},{4,0},{6,2},{8,12},{10,14},{12,8},{14,10},{16,20},{18,... | collective-permute-start | bytes 884744 | tf_op jit(solution)/shard_map/ppermute | solution.py:187
  15.7 25.5 %collective-permute-start.6 = (bf16[4,144,256]{2,1,0:T(8,128)(2,1)S(1)}, bf16[4,144,256]{2,1,0:T(8,128)(2,1)}, u32[]{:S(2)}, u32[]{:S(2)}) collective-permute-start(bf16[4,144,256]{2,1,0:T(8,128)(2,1)S(1)} %constant_dynamic-update-slice_fusion.refs_0_), channel_id=1, source_target_pairs={{0,6},{2,4},{4,2},{6,0},{8,14},{10,12},{12,10},{14,8},{16,22},{18,... | collective-permute-start | bytes 884744 | tf_op jit(solution)/shard_map/ppermute | solution.py:187
  16.1 9.7 %collective-permute-start.7 = (f32[4,64,256]{2,1,0:T(8,128)S(1)}, f32[4,64,256]{2,1,0:T(8,128)S(1)}, u32[]{:S(2)}, u32[]{:S(2)}) collective-permute-start(f32[4,64,256]{2,1,0:T(8,128)S(1)} %constant_dynamic-slice_fusion.2), channel_id=1, source_target_pairs={{0,1},{1,0},{2,3},{3,2},{4,5},{5,4},{6,7},{7,6},{8,9},{9,8},{10,11... | collective-permute-start | bytes 786440 | tf_op jit(solution)/shard_map/ppermute | solution.py:247
  41.2 21.6 %copy-start.4 = (s32[4,6]{1,0:T(4,128)S(1)}, s32[4,6]{1,0:T(4,128)}, u32[]{:S(2)}) copy-start(s32[4,6]{1,0:T(4,128)} %owners.1) | copy-start | bytes 292
  43.0 7.0 %collective-permute-start.8 = (bf16[16,48,256]{2,1,0:T(8,128)(2,1)}, bf16[16,48,256]{2,1,0:T(8,128)(2,1)}, u32[]{:S(2)}, u32[]{:S(2)}) collective-permute-start(bf16[16,48,256]{2,1,0:T(8,128)(2,1)} %ends.1), channel_id=1, source_target_pairs={{0,1},{1,0},{2,3},{3,2},{4,5},{5,4},{6,7},{7,6},{8,9},{9,8},{10,11... | collective-permute-start | bytes 1179656 | tf_op jit(solution)/shard_map/ppermute | solution.py:247
  58.5 4.3 %collective-permute-start.9 = (bf16[32,48,256]{2,1,0:T(8,128)(2,1)S(1)}, bf16[32,48,256]{2,1,0:T(8,128)(2,1)}, u32[]{:S(2)}, u32[]{:S(2)}) collective-permute-start(bf16[32,48,256]{2,1,0:T(8,128)(2,1)S(1)} %constant_dynamic-slice_fusion.1), channel_id=1, source_target_pairs={{0,1},{1,0},{2,3},{3,2},{4,5},{5,4},{6,7},{7,6},{8,9},{9,8},{10,11... | collective-permute-start | bytes 2359304 | tf_op jit(solution)/shard_map/ppermute | solution.py:247

commit v2 on v1

--- a/solution.py
+++ b/solution.py
@@ -409,6 +409,8 @@
     for more in range(GROUP - 1):
         lists[main_slot + in_main + more] = lists[main_slot]
         lists[main_code + in_main + more] = blank
+        lists[third_slot + in_third + more] = lists[third_slot]
+        lists[third_source + in_third + more] = lists[third_source]
         lists[third_code + in_third + more] = blank
 
 
@@ -441,10 +443,11 @@
     sources, out, refs = refs[:number], refs[number], refs[number + 1 :]
     copied, refs = refs[:number], refs[number:]
     bands_of, main_halo = copied[: 2 * ITERS], copied[2 * ITERS :]
-    lists, held, recip, following, total, result, own_sems, held_sems, out_sems, lists_sem = refs
+    lists, held, *refs = refs
+    held_halo, refs = refs[:sides], refs[sides:]
+    recip, following, total, result, own_sems, held_sems, out_sems, lists_sem = refs
     blocks, depth, lat = out.shape
     nviews = bands_of[0].shape[0]
-    per_part = parts[0].shape[0]
     own = [
         pltpu.make_async_copy(source, to, own_sems.at[k])
         for k, (source, to) in enumerate(zip(sources, copied))
@@ -454,33 +457,16 @@
     listing.start()
     for copy in own[1:]:
         copy.start()
-    listing.wait()
-
-    mains, thirds = lists[numbers], lists[numbers + 1]
-    low = pl.multiple_of(lists[numbers + 2], H)
-    counts = [lists[numbers + 3 + b] for b in range(blocks)]
-    def copies(p, part, at, slot):
-        yield pltpu.make_async_copy(
-            part.at[at, pl.ds(0, depth)], held.at[p, pl.ds(0, depth)], held_sems.at[p, 0]
+    number, part_rows = parts[0].shape[0], parts[0].shape[1]
+    third_copies = [
+        pltpu.make_async_copy(
+            part, held.at[pl.ds(j * number, number), pl.ds(0, part_rows)], held_sems.at[j]
         )
-        for side, ref in enumerate(third_halo):
-            rows = pl.ds(depth + side * VIEW_HALO, VIEW_HALO)
-            yield pltpu.make_async_copy(ref.at[slot], held.at[p, rows], held_sems.at[p, 1 + side])
-
-    @pl.loop(0, thirds)
-    def _(p):
-        slot = lists[third_slot + p]
-        for j, part in enumerate(parts):
-
-            @pl.when(jnp.logical_and(slot >= j * per_part, slot < (j + 1) * per_part))
-            def _():
-                for copy in copies(p, part, slot - j * per_part, slot):
-                    copy.start()
-
-    @pl.loop(thirds, (thirds + (GROUP - 1)) // GROUP * GROUP)
-    def _(p):
-        held[p] = jnp.zeros(held.shape[1:], held.dtype)
-
+        for j, part in enumerate(parts)
+    ] + [
+        pltpu.make_async_copy(ref, to, held_sems.at[nparts + side])
+        for side, (ref, to) in enumerate(zip(third_halo, held_halo))
+    ]
     recip[blocks * nviews] = jnp.zeros(recip.shape[1:], recip.dtype)
     stores = []
     for sweep in range(ITERS):
@@ -488,8 +474,6 @@
         forward, mirror = bands_of[2 * sweep], bands_of[2 * sweep + 1]
         next_rows, view_rows = mirror.shape[1], mirror.shape[2]
         side_rows = halo_rows(sweep)
-        next_at = pl.multiple_of(2 * low, 2 * H)
-        halo_at = [pl.multiple_of(2 * sweep * low, 2 * H), 0]
         own[2 * sweep].wait()
         for b in range(blocks):
             rounded = current[b, : forward.shape[2]].astype(jnp.bfloat16)
@@ -500,6 +484,19 @@
                     inverse = jnp.where(blurred > 0, inverse, 0.0)
                 recip[b * nviews + v, :view_rows] = inverse
 
+        if sweep == 0:
+            listing.wait()
+            mains, thirds = lists[numbers], lists[numbers + 1]
+            low = pl.multiple_of(lists[numbers + 2], H)
+            counts = [lists[numbers + 3 + b] for b in range(blocks)]
+
+            @pl.when(thirds > 0)
+            def _():
+                for copy in third_copies:
+                    copy.start()
+
+        next_at = pl.multiple_of(2 * low, 2 * H)
+        halo_at = [pl.multiple_of(2 * sweep * low, 2 * H), 0]
         total[:, :next_rows] = jnp.zeros((blocks + 1, next_rows, lat), jnp.float32)
 
         def main_rows(p):
@@ -510,10 +507,10 @@
             return rows
 
         def third_rows(p):
-            rows = [held[p, :depth]]
-            for side in range(sides):
-                at = depth + side * VIEW_HALO + halo_at[side]
-                rows.append(held[p, pl.ds(pl.multiple_of(at, H), side_rows)])
+            slot = lists[third_slot + p]
+            rows = [held[slot, :depth]]
+            for side, ref in enumerate(held_halo):
+                rows.append(ref[slot, pl.ds(halo_at[side], side_rows)])
             return rows
 
         def add(number, rows_of, code_at):
@@ -546,9 +543,9 @@
         add(mains, main_rows, main_code)
         if sweep == 0:
 
-            @pl.loop(0, thirds)
-            def _(p):
-                for copy in copies(p, parts[0], 0, 0):
+            @pl.when(thirds > 0)
+            def _():
+                for copy in third_copies:
                     copy.wait()
 
         add(thirds, third_rows, third_code)
@@ -571,8 +568,8 @@
     blocks, frame, lat = est.shape
     nviews, view_rows = matrices[0].shape[:2]
     sides = len(main_halo)
-    thirds = parts[0].shape[0] * len(parts) + GROUP
     following = (frame - 2 * sides * H, lat)
+    third_halo_shape = (len(parts) * parts[0].shape[0], VIEW_HALO, lat)
     copied = [*matrices, *main_halo]
     in_place = [*parts, *third_halo, *copied]
     return pl.pallas_call(
@@ -583,13 +580,16 @@
         scratch_shapes=[pltpu.VMEM(array.shape, array.dtype) for array in copied]
         + [
             pltpu.SMEM(lists.shape, lists.dtype),
-            pltpu.VMEM((thirds, view_rows, lat), jnp.bfloat16),
+            pltpu.VMEM((third_halo_shape[0], depth + TILE, lat), main.dtype),
+        ]
+        + [pltpu.VMEM(third_halo_shape, main.dtype)] * sides
+        + [
             pltpu.VMEM((blocks * nviews + 1, view_rows, lat), jnp.float32),
             pltpu.VMEM((blocks, *following), jnp.float32),
             pltpu.VMEM((blocks + 1, *following), jnp.float32),
             pltpu.VMEM((blocks, depth, lat), jnp.float32),
             pltpu.SemaphoreType.DMA((len(copied),)),
-            pltpu.SemaphoreType.DMA((thirds, 1 + sides)),
+            pltpu.SemaphoreType.DMA((len(parts) + sides,)),
             pltpu.SemaphoreType.DMA((blocks,)),
             pltpu.SemaphoreType.DMA,
         ],

time: 70.3 us -> 69.7 us (level)
  the two profiles are of different devices: /device:TPU:17 before, /device:TPU:13 now
where the time goes in v2:
time: 69.7 us; the launch traced here: 69.2 us
  waiting for transfers between devices  23.6 us (34%)
  Pallas kernels  20.7 us (30%)
  starting transfers between devices  20 us (29%)
  other arithmetic  3.21 us (5%)
  local copies, waits for them, and re-layouts  0.89 us (1%)
  between operations  0.82 us (1%)
    all_to_all x1, waiting for transfers between devices, local(): lax.all_to_all(packed.reshape(peers, MAIN, depth, lat), 'join', split_axi...  11.5 us
    ppermute x3, waiting for transfers between devices, among_members(): parts.append(lax.ppermute(line, 'join', [(i, i ^ m) for i in range(peers)]))  10.8 us
    ppermute x3, starting transfers between devices, halos(): return [lax.ppermute(sent, 'view', [(0, 1), (1, 0)])]  8.75 us
    pallas_call x1, Pallas kernels, bands(): pl.pallas_call(functools.partial(bands_kernel, shapes), out_shape=outs, i...  6.11 us
    pallas_call x1, Pallas kernels, deconvolve(): pl.pallas_call(functools.partial(deconvolve_kernel, starts, len(parts), s...  5.61 us
    all_to_all x1, starting transfers between devices, local(): lax.all_to_all(packed.reshape(peers, MAIN, depth, lat), 'join', split_axi...  4.7 us
    pallas_call x1, Pallas kernels, plan(): pl.pallas_call(functools.partial(plan_kernel, nviews, blocks), out_shape=...  3.91 us
    ppermute x3, starting transfers between devices, along_groups(): lax.ppermute(rows[k], 'join', [(i, (i + k * members) % peers) for i in ra...  3.84 us
  transfers between devices with their start and end apart: 10, of which 3 were waited for; matrix products, arithmetic and copies ran while one was open for 6% of the time, Pallas kernels for 17%

profile of v2, /device:TPU:13, one launch (start us, length us, event | category | flops | bytes accessed | tf_op | source)
XLA Modules:
  0.0 69.2 jit_solution(16582754119688704198)
XLA Ops:
  0.0 3.3 %pack.1 = (bf16[32,128,256]{2,1,0:T(8,128)(2,1)}, bf16[1,144,256]{2,1,0:T(8,128)(2,1)}, bf16[1,144,256]{2,1,0:T(8,128)(2,1)}, bf16[1,144,256]{2,1,0:T(8,128)(2,1)}, bf16[1,144,256]{2,1,0:T(8,128)(2,1)}) custom-call(s32[4,6]{1,0:T(4,128)} %owners.1, s32[4,6]{1,0:T(4,128)} %blocks_of.1, s32[1]{0:T(128)} %bitcast.here, bf16[4,6,128,256]{3,2,1,0:T(8,128)(2,1)} %views.1), custom_call_target="tpu_custom_call" | custom-call | tf_op jit(solution)/shard_map/pack/pallas_call | solution.py:104
  3.3 1.3 %collective-permute-start.1 = (bf16[1,144,256]{2,1,0:T(8,128)(2,1)}, bf16[1,144,256]{2,1,0:T(8,128)(2,1)S(1)}, u32[]{:S(2)}, u32[]{:S(2)}) collective-permute-start(bf16[1,144,256]{2,1,0:T(8,128)(2,1)} %get-tuple-element.115), channel_id=1, source_target_pairs={{0,8},{2,10},{4,12},{6,14},{8,16},{10,18},{12,20},{14,22},{16,24},... | collective-permute-start | bytes 221192 | tf_op jit(solution)/shard_map/ppermute | solution.py:176
  4.6 1.1 %collective-permute-start.2 = (bf16[1,144,256]{2,1,0:T(8,128)(2,1)}, bf16[1,144,256]{2,1,0:T(8,128)(2,1)S(1)}, u32[]{:S(2)}, u32[]{:S(2)}) collective-permute-start(bf16[1,144,256]{2,1,0:T(8,128)(2,1)} %get-tuple-element.116), channel_id=1, source_target_pairs={{0,16},{2,18},{4,20},{6,22},{8,24},{10,26},{12,28},{14,30},{16,0},... | collective-permute-start | bytes 221192 | tf_op jit(solution)/shard_map/ppermute | solution.py:176
  5.7 1.4 %collective-permute-start.3 = (bf16[1,144,256]{2,1,0:T(8,128)(2,1)}, bf16[1,144,256]{2,1,0:T(8,128)(2,1)S(1)}, u32[]{:S(2)}, u32[]{:S(2)}) collective-permute-start(bf16[1,144,256]{2,1,0:T(8,128)(2,1)} %get-tuple-element.117), channel_id=1, source_target_pairs={{0,24},{2,26},{4,28},{6,30},{8,0},{10,2},{12,4},{14,6},{16,8},{18,... | collective-permute-start | bytes 221192 | tf_op jit(solution)/shard_map/ppermute | solution.py:176
  7.1 0.0 copy-start.3
  7.1 0.0 copy-start.2
  7.1 0.0 copy-start.1
  7.1 4.7 %all-to-all-start.1 = ((bf16[16,2,128,256]{3,2,1,0:T(8,128)(2,1)}), bf16[16,2,128,256]{3,2,1,0:T(8,128)(2,1)S(1)}, u32[]{:S(2)}, u32[]{:S(2)}) async-start(bf16[16,2,128,256]{3,2,1,0:T(8,128)(2,1)} %bitcast.17), calls=%async_computation.1 | async-start | bytes 4194304 | tf_op jit(solution)/shard_map/all_to_all | solution.py:614
  11.8 0.0 copy-done.3
  11.8 0.1 reduce_sum.9
  11.9 0.1 divide_convert_fusion
  12.0 0.0 copy-done.2
  12.0 0.7 stack.44.shifts
  12.7 0.5 fusion.5.source
  13.3 0.0 collective-permute-done.1
  13.3 0.0 collective-permute-done.2
  13.3 0.0 collective-permute-done.3
  13.3 1.2 %collective-permute-start.4 = (bf16[4,144,256]{2,1,0:T(8,128)(2,1)S(1)}, bf16[4,144,256]{2,1,0:T(8,128)(2,1)}, u32[]{:S(2)}, u32[]{:S(2)}) collective-permute-start(bf16[4,144,256]{2,1,0:T(8,128)(2,1)S(1)} %constant_dynamic-update-slice_fusion.refs_0_), channel_id=1, source_target_pairs={{0,2},{2,0},{4,6},{6,4},{8,10},{10,8},{12,14},{14,12},{16,18},{18,... | collective-permute-start | bytes 884744 | tf_op jit(solution)/shard_map/ppermute | solution.py:187
  14.6 0.3 collective-permute-start.5
  14.9 1.2 %collective-permute-start.6 = (bf16[4,144,256]{2,1,0:T(8,128)(2,1)S(1)}, bf16[4,144,256]{2,1,0:T(8,128)(2,1)}, u32[]{:S(2)}, u32[]{:S(2)}) collective-permute-start(bf16[4,144,256]{2,1,0:T(8,128)(2,1)S(1)} %constant_dynamic-update-slice_fusion.refs_0_), channel_id=1, source_target_pairs={{0,6},{2,4},{4,2},{6,0},{8,14},{10,12},{12,10},{14,8},{16,22},{18,... | collective-permute-start | bytes 884744 | tf_op jit(solution)/shard_map/ppermute | solution.py:187
  16.0 0.1 rev.3
  16.1 0.0 copy-done.1
  16.2 3.0 %collective-permute-start.7 = (f32[4,64,256]{2,1,0:T(8,128)S(1)}, f32[4,64,256]{2,1,0:T(8,128)S(1)}, u32[]{:S(2)}, u32[]{:S(2)}) collective-permute-start(f32[4,64,256]{2,1,0:T(8,128)S(1)} %constant_dynamic-slice_fusion.2), channel_id=1, source_target_pairs={{0,1},{1,0},{2,3},{3,2},{4,5},{5,4},{6,7},{7,6},{8,9},{9,8},{10,11... | collective-permute-start | bytes 786440 | tf_op jit(solution)/shard_map/ppermute | solution.py:247
  19.1 0.6 fusion.3.taps_rows
  19.7 6.1 %bands.1 = (bf16[6,176,192]{2,1,0:T(8,128)(2,1)}, bf16[6,160,176]{2,1,0:T(8,128)(2,1)}, bf16[6,144,160]{2,1,0:T(8,128)(2,1)}, bf16[6,128,144]{2,1,0:T(8,128)(2,1)}) custom-call(s32[8]{0:T(128)} %stack.44.shifts, f32[2,6,256]{2,1,0:T(8,128)} %fusion.3.taps_rows), custom_call_target="tpu_custom_call" | custom-call | flops 99999997952 | tf_op jit(solution)/shard_map/bands/pallas_call | solution.py:335
  25.9 0.0 collective-permute-done.7
  25.9 1.3 %maximum_select_fusion = f32[4,192,256]{2,1,0:T(8,128)S(1)} fusion(f32[4,64,256]{2,1,0:T(8,128)S(1)} %collective-permute-done.7, f32[4,128,256]{2,1,0:T(8,128)} %param.7, pred[]{:T(512)S(6)} %eq.4), kind=kLoop, calls=%fused_computation.1 | loop fusion | flops 589824 | bytes 1572865 | tf_op jit(solution)/shard_map/jit(_where)/select_n | solution.py:261
  27.2 0.0 collective-permute-done.4.refs_1_
  27.2 10.8 %collective-permute-done.5.refs_2_ = bf16[4,144,256]{2,1,0:T(8,128)(2,1)} collective-permute-done((bf16[4,144,256]{2,1,0:T(8,128)(2,1)S(1)}, bf16[4,144,256]{2,1,0:T(8,128)(2,1)}, u32[]{:S(2)}, u32[]{:S(2)}) %collective-permute-start.5) | collective-permute-done | bytes 294944 | tf_op jit(solution)/shard_map/ppermute | solution.py:187
  38.0 0.0 collective-permute-done.6.refs_3_
  38.0 0.0 copy-start.4
  38.0 1.8 %ends.1 = bf16[16,48,256]{2,1,0:T(8,128)(2,1)} custom-call(s32[1]{0:T(128)} %bitcast.10.start, bf16[4,144,256]{2,1,0:T(8,128)(2,1)S(1)} %constant_dynamic-update-slice_fusion.refs_0_, bf16[4,144,256]{2,1,0:T(8,128)(2,1)} %collective-permute-done.4.refs_1_, bf16[4,144,256]{2,1,0:T(8,128)(2,1)} %collective-permute-done.5.refs_2_, ...), custom_call_target="tpu_custom_call" | custom-call | tf_op jit(solution)/shard_map/ends/pallas_call | solution.py:228
  39.7 4.2 %collective-permute-start.8 = (bf16[16,48,256]{2,1,0:T(8,128)(2,1)}, bf16[16,48,256]{2,1,0:T(8,128)(2,1)}, u32[]{:S(2)}, u32[]{:S(2)}) collective-permute-start(bf16[16,48,256]{2,1,0:T(8,128)(2,1)} %ends.1), channel_id=1, source_target_pairs={{0,1},{1,0},{2,3},{3,2},{4,5},{5,4},{6,7},{7,6},{8,9},{9,8},{10,11... | collective-permute-start | bytes 1179656 | tf_op jit(solution)/shard_map/ppermute | solution.py:247
  44.0 0.6 pad_add_fusion.place
  44.6 3.9 %plan.1 = (s32[199]{0:T(256)S(1)}, s32[1]{0:T(128)}) custom-call(s32[2]{0:T(128)} %pad_add_fusion.place, s32[16]{0:T(128)} %fusion.5.source, bf16[4,144,256]{2,1,0:T(8,128)(2,1)S(1)} %constant_dynamic-update-slice_fusion.refs_0_, bf16[4,144,256]{2,1,0:T(8,128)(2,1)} %collective-permute-done.4.refs_1_, bf16[4,144,256]{2,1,0:T(8,128)(2,1)} %collective-permute-done.5.refs_2_, ...), custom_call_target="tpu_custom_call" | custom-call | tf_op jit(solution)/shard_map/plan/pallas_call | solution.py:421
  48.5 0.0 collective-permute-done.8
  48.5 11.5 %all-to-all-done.1 = bf16[16,2,128,256]{3,2,1,0:T(8,128)(2,1)S(1)} async-done(((bf16[16,2,128,256]{3,2,1,0:T(8,128)(2,1)}), bf16[16,2,128,256]{3,2,1,0:T(8,128)(2,1)S(1)}, u32[]{:S(2)}, u32[]{:S(2)}) %all-to-all-start.1) | async-done | bytes 2097184 | tf_op jit(solution)/shard_map/all_to_all | solution.py:614
  60.0 0.1 constant_dynamic-slice_fusion.1
  60.0 1.5 %collective-permute-start.9 = (bf16[32,48,256]{2,1,0:T(8,128)(2,1)S(1)}, bf16[32,48,256]{2,1,0:T(8,128)(2,1)}, u32[]{:S(2)}, u32[]{:S(2)}) collective-permute-start(bf16[32,48,256]{2,1,0:T(8,128)(2,1)S(1)} %constant_dynamic-slice_fusion.1), channel_id=1, source_target_pairs={{0,1},{1,0},{2,3},{3,2},{4,5},{5,4},{6,7},{7,6},{8,9},{9,8},{10,11... | collective-permute-start | bytes 2359304 | tf_op jit(solution)/shard_map/ppermute | solution.py:247
  62.2 1.3 %collective-permute-done.9 = bf16[32,48,256]{2,1,0:T(8,128)(2,1)} collective-permute-done((bf16[32,48,256]{2,1,0:T(8,128)(2,1)S(1)}, bf16[32,48,256]{2,1,0:T(8,128)(2,1)}, u32[]{:S(2)}, u32[]{:S(2)}) %collective-permute-start.9) | collective-permute-done | bytes 786464 | tf_op jit(solution)/shard_map/ppermute | solution.py:247
  63.6 0.0 copy-done.4
  63.6 5.6 %conditional.1 = (f32[4,128,256]{2,1,0:T(8,128)}) conditional(s32[]{:T(128)} %bitcast.13, (s32[199]{0:T(256)S(1)}, bf16[32,128,256]{2,1,0:T(8,128)(2,1)S(1)}, f32[4,192,256]{2,1,0:T(8,128)S(1)}, bf16[4,144,256]{2,1,0:T(8,128)(2,1)S(1)}, bf16[4,144,256]{2,1,0:T(8,128)(2,1)}, /*index=5*/bf16[4,144,256]{2,1,0:T(8,128)(2,1)}, ...), branch_computations={%region_1.2_spmd, %region_2.3_spmd} | conditional | flops 4 | bytes 8650906 | solution.py:655
  63.6 5.6 %deconvolve.2 = f32[4,128,256]{2,1,0:T(8,128)} custom-call(s32[199]{0:T(256)S(1)} %get-tuple-element.54.listed, bf16[32,128,256]{2,1,0:T(8,128)(2,1)S(1)} %get-tuple-element.55.main, f32[4,192,256]{2,1,0:T(8,128)S(1)} %get-tuple-element.56.est, bf16[4,144,256]{2,1,0:T(8,128)(2,1)S(1)} %get-tuple-element.57.refs_0_, ...), custom_call_target="tpu_custom_call" | custom-call | tf_op jit(solution)/shard_map/cond/branch_0_fun/deconvolve/pallas_call | solution.py:575
  (5 shorter events, 0.0 us)
Async XLA Ops:
  3.3 10.0 %collective-permute-start.1 = (bf16[1,144,256]{2,1,0:T(8,128)(2,1)}, bf16[1,144,256]{2,1,0:T(8,128)(2,1)S(1)}, u32[]{:S(2)}, u32[]{:S(2)}) collective-permute-start(bf16[1,144,256]{2,1,0:T(8,128)(2,1)} %get-tuple-element.115), channel_id=1, source_target_pairs={{0,8},{2,10},{4,12},{6,14},{8,16},{10,18},{12,20},{14,22},{16,24},... | collective-permute-start | bytes 221192 | tf_op jit(solution)/shard_map/ppermute | solution.py:176
  4.6 8.7 %collective-permute-start.2 = (bf16[1,144,256]{2,1,0:T(8,128)(2,1)}, bf16[1,144,256]{2,1,0:T(8,128)(2,1)S(1)}, u32[]{:S(2)}, u32[]{:S(2)}) collective-permute-start(bf16[1,144,256]{2,1,0:T(8,128)(2,1)} %get-tuple-element.116), channel_id=1, source_target_pairs={{0,16},{2,18},{4,20},{6,22},{8,24},{10,26},{12,28},{14,30},{16,0},... | collective-permute-start | bytes 221192 | tf_op jit(solution)/shard_map/ppermute | solution.py:176
  5.7 7.6 %collective-permute-start.3 = (bf16[1,144,256]{2,1,0:T(8,128)(2,1)}, bf16[1,144,256]{2,1,0:T(8,128)(2,1)S(1)}, u32[]{:S(2)}, u32[]{:S(2)}) collective-permute-start(bf16[1,144,256]{2,1,0:T(8,128)(2,1)} %get-tuple-element.117), channel_id=1, source_target_pairs={{0,24},{2,26},{4,28},{6,30},{8,0},{10,2},{12,4},{14,6},{16,8},{18,... | collective-permute-start | bytes 221192 | tf_op jit(solution)/shard_map/ppermute | solution.py:176
  7.1 4.7 %copy-start.3 = (f32[6,33]{1,0:T(8,128)S(1)}, f32[6,33]{1,0:T(8,128)}, u32[]{:S(2)}) copy-start(f32[6,33]{1,0:T(8,128)} %param.11) | copy-start | bytes 2380
  7.1 4.9 %copy-start.2 = (bf16[1,144,256]{2,1,0:T(8,128)(2,1)S(1)}, bf16[1,144,256]{2,1,0:T(8,128)(2,1)}, u32[]{:S(2)}) copy-start(bf16[1,144,256]{2,1,0:T(8,128)(2,1)} %get-tuple-element.114) | copy-start | bytes 221188
  7.1 9.0 %copy-start.1 = (f32[4,128,256]{2,1,0:T(8,128)S(1)}, f32[4,128,256]{2,1,0:T(8,128)}, u32[]{:S(2)}) copy-start(f32[4,128,256]{2,1,0:T(8,128)} %param.7) | copy-start | bytes 1572868
  7.1 52.8 %all-to-all-start.1 = ((bf16[16,2,128,256]{3,2,1,0:T(8,128)(2,1)}), bf16[16,2,128,256]{3,2,1,0:T(8,128)(2,1)S(1)}, u32[]{:S(2)}, u32[]{:S(2)}) async-start(bf16[16,2,128,256]{3,2,1,0:T(8,128)(2,1)} %bitcast.17), calls=%async_computation.1 | async-start | bytes 4194304 | tf_op jit(solution)/shard_map/all_to_all | solution.py:614
  13.3 13.8 %collective-permute-start.4 = (bf16[4,144,256]{2,1,0:T(8,128)(2,1)S(1)}, bf16[4,144,256]{2,1,0:T(8,128)(2,1)}, u32[]{:S(2)}, u32[]{:S(2)}) collective-permute-start(bf16[4,144,256]{2,1,0:T(8,128)(2,1)S(1)} %constant_dynamic-update-slice_fusion.refs_0_), channel_id=1, source_target_pairs={{0,2},{2,0},{4,6},{6,4},{8,10},{10,8},{12,14},{14,12},{16,18},{18,... | collective-permute-start | bytes 884744 | tf_op jit(solution)/shard_map/ppermute | solution.py:187
  14.6 23.4 %collective-permute-start.5 = (bf16[4,144,256]{2,1,0:T(8,128)(2,1)S(1)}, bf16[4,144,256]{2,1,0:T(8,128)(2,1)}, u32[]{:S(2)}, u32[]{:S(2)}) collective-permute-start(bf16[4,144,256]{2,1,0:T(8,128)(2,1)S(1)} %constant_dynamic-update-slice_fusion.refs_0_), channel_id=1, source_target_pairs={{0,4},{2,6},{4,0},{6,2},{8,12},{10,14},{12,8},{14,10},{16,20},{18,... | collective-permute-start | bytes 884744 | tf_op jit(solution)/shard_map/ppermute | solution.py:187
  14.9 23.1 %collective-permute-start.6 = (bf16[4,144,256]{2,1,0:T(8,128)(2,1)S(1)}, bf16[4,144,256]{2,1,0:T(8,128)(2,1)}, u32[]{:S(2)}, u32[]{:S(2)}) collective-permute-start(bf16[4,144,256]{2,1,0:T(8,128)(2,1)S(1)} %constant_dynamic-update-slice_fusion.refs_0_), channel_id=1, source_target_pairs={{0,6},{2,4},{4,2},{6,0},{8,14},{10,12},{12,10},{14,8},{16,22},{18,... | collective-permute-start | bytes 884744 | tf_op jit(solution)/shard_map/ppermute | solution.py:187
  16.2 9.7 %collective-permute-start.7 = (f32[4,64,256]{2,1,0:T(8,128)S(1)}, f32[4,64,256]{2,1,0:T(8,128)S(1)}, u32[]{:S(2)}, u32[]{:S(2)}) collective-permute-start(f32[4,64,256]{2,1,0:T(8,128)S(1)} %constant_dynamic-slice_fusion.2), channel_id=1, source_target_pairs={{0,1},{1,0},{2,3},{3,2},{4,5},{5,4},{6,7},{7,6},{8,9},{9,8},{10,11... | collective-permute-start | bytes 786440 | tf_op jit(solution)/shard_map/ppermute | solution.py:247
  38.0 25.6 %copy-start.4 = (s32[4,6]{1,0:T(4,128)S(1)}, s32[4,6]{1,0:T(4,128)}, u32[]{:S(2)}) copy-start(s32[4,6]{1,0:T(4,128)} %owners.1) | copy-start | bytes 292
  39.7 8.8 %collective-permute-start.8 = (bf16[16,48,256]{2,1,0:T(8,128)(2,1)}, bf16[16,48,256]{2,1,0:T(8,128)(2,1)}, u32[]{:S(2)}, u32[]{:S(2)}) collective-permute-start(bf16[16,48,256]{2,1,0:T(8,128)(2,1)} %ends.1), channel_id=1, source_target_pairs={{0,1},{1,0},{2,3},{3,2},{4,5},{5,4},{6,7},{7,6},{8,9},{9,8},{10,11... | collective-permute-start | bytes 1179656 | tf_op jit(solution)/shard_map/ppermute | solution.py:247
  60.0 3.6 %collective-permute-start.9 = (bf16[32,48,256]{2,1,0:T(8,128)(2,1)S(1)}, bf16[32,48,256]{2,1,0:T(8,128)(2,1)}, u32[]{:S(2)}, u32[]{:S(2)}) collective-permute-start(bf16[32,48,256]{2,1,0:T(8,128)(2,1)S(1)} %constant_dynamic-slice_fusion.1), channel_id=1, source_target_pairs={{0,1},{1,0},{2,3},{3,2},{4,5},{5,4},{6,7},{7,6},{8,9},{9,8},{10,11... | collective-permute-start | bytes 2359304 | tf_op jit(solution)/shard_map/ppermute | solution.py:247

commit v3 on v2

--- a/solution.py
+++ b/solution.py
@@ -11,7 +11,8 @@
 CAP = 3
 MAIN = 2
 ITERS = 2
-GROUP = 16
+GROUP = 32
+SMALL = 16
 TILE = 16
 EST_HALO = 2 * ITERS * H
 VIEW_HALO = EST_HALO - H
@@ -475,7 +476,13 @@
         next_rows, view_rows = mirror.shape[1], mirror.shape[2]
         side_rows = halo_rows(sweep)
         own[2 * sweep].wait()
-        for b in range(blocks):
+        seen_blocks = range(blocks)
+        if sweep > 0 and blocks > 2:
+            unseen = jnp.int32(blocks - 2)
+            for b in reversed(range(1, blocks - 2)):
+                unseen = jnp.where(counts[b] == 0, b, unseen)
+            seen_blocks = [b + (b >= unseen).astype(jnp.int32) for b in range(blocks - 1)]
+        for b in seen_blocks:
             rounded = current[b, : forward.shape[2]].astype(jnp.bfloat16)
             for v in range(nviews):
                 blurred = jnp.dot(forward[v], rounded, preferred_element_type=jnp.float32)
@@ -514,27 +521,33 @@
             return rows
 
         def add(number, rows_of, code_at):
-            @pl.loop(0, (number + (GROUP - 1)) // GROUP)
-            def _(group):
-                gained = []
-                for member in range(GROUP):
-                    p = group * GROUP + member
-                    code = lists[code_at + p]
-                    b = code // nviews
-                    pieces, first = [], 0
-                    for rows in rows_of(p):
-                        last = first + rows.shape[0]
-                        quotient = rows.astype(jnp.float32) * recip[code, first:last]
-                        pieces.append(quotient.astype(jnp.bfloat16))
-                        first = last
-                    part = jnp.dot(
-                        mirror[code - b * nviews],
-                        jnp.concatenate(pieces, axis=0),
-                        preferred_element_type=jnp.float32,
-                    )
-                    gained.append((b, part))
-                for b, part in gained:
-                    total[b, :next_rows] += part
+            wide = (number + (SMALL - 1)) // GROUP
+            pl.loop(0, wide)(lambda group: add_group(group * GROUP, GROUP, rows_of, code_at))
+
+            @pl.when(number > wide * GROUP)
+            def _():
+                add_group(wide * GROUP, SMALL, rows_of, code_at)
+
+        def add_group(first_entry, size, rows_of, code_at):
+            gained = []
+            for member in range(size):
+                p = first_entry + member
+                code = lists[code_at + p]
+                b = code // nviews
+                pieces, first = [], 0
+                for rows in rows_of(p):
+                    last = first + rows.shape[0]
+                    quotient = rows.astype(jnp.float32) * recip[code, first:last]
+                    pieces.append(quotient.astype(jnp.bfloat16))
+                    first = last
+                part = jnp.dot(
+                    mirror[code - b * nviews],
+                    jnp.concatenate(pieces, axis=0),
+                    preferred_element_type=jnp.float32,
+                )
+                gained.append((b, part))
+            for b, part in gained:
+                total[b, :next_rows] += part
 
         own[2 * sweep + 1].wait()
         if sweep == 0:

time: 69.7 us -> 70.1 us (level)
  no operation moved by 1% of the time
where the time goes in v3:
time: 70.1 us; the launch traced here: 69.4 us
  waiting for transfers between devices  23.5 us (34%)
  Pallas kernels  20.7 us (30%)
  starting transfers between devices  19.9 us (28%)
  other arithmetic  3.22 us (5%)
  between operations  1 us (1%)
  local copies, waits for them, and re-layouts  0.89 us (1%)
    all_to_all x1, waiting for transfers between devices, local(): lax.all_to_all(packed.reshape(peers, MAIN, depth, lat), 'join', split_axi...  11.3 us
    ppermute x3, waiting for transfers between devices, among_members(): parts.append(lax.ppermute(line, 'join', [(i, i ^ m) for i in range(peers)]))  10.9 us
    ppermute x3, starting transfers between devices, halos(): return [lax.ppermute(sent, 'view', [(0, 1), (1, 0)])]  8.66 us
    pallas_call x1, Pallas kernels, bands(): pl.pallas_call(functools.partial(bands_kernel, shapes), out_shape=outs, i...  6.11 us
    pallas_call x1, Pallas kernels, deconvolve(): pl.pallas_call(functools.partial(deconvolve_kernel, starts, len(parts), s...  5.38 us
    all_to_all x1, starting transfers between devices, local(): lax.all_to_all(packed.reshape(peers, MAIN, depth, lat), 'join', split_axi...  4.69 us
    pallas_call x1, Pallas kernels, plan(): pl.pallas_call(functools.partial(plan_kernel, nviews, blocks), out_shape=...  4.1 us
    ppermute x3, starting transfers between devices, along_groups(): lax.ppermute(rows[k], 'join', [(i, (i + k * members) % peers) for i in ra...  3.81 us
  transfers between devices with their start and end apart: 10, of which 3 were waited for; matrix products, arithmetic and copies ran while one was open for 6% of the time, Pallas kernels for 17%

profile of v3, /device:TPU:13, one launch (start us, length us, event | category | flops | bytes accessed | tf_op | source)
XLA Modules:
  0.0 69.4 jit_solution(2632068750544955497)
XLA Ops:
  0.0 3.3 %pack.1 = (bf16[32,128,256]{2,1,0:T(8,128)(2,1)}, bf16[1,144,256]{2,1,0:T(8,128)(2,1)}, bf16[1,144,256]{2,1,0:T(8,128)(2,1)}, bf16[1,144,256]{2,1,0:T(8,128)(2,1)}, bf16[1,144,256]{2,1,0:T(8,128)(2,1)}) custom-call(s32[4,6]{1,0:T(4,128)} %owners.1, s32[4,6]{1,0:T(4,128)} %blocks_of.1, s32[1]{0:T(128)} %bitcast.here, bf16[4,6,128,256]{3,2,1,0:T(8,128)(2,1)} %views.1), custom_call_target="tpu_custom_call" | custom-call | tf_op jit(solution)/shard_map/pack/pallas_call | solution.py:105
  3.3 1.3 %collective-permute-start.1 = (bf16[1,144,256]{2,1,0:T(8,128)(2,1)}, bf16[1,144,256]{2,1,0:T(8,128)(2,1)S(1)}, u32[]{:S(2)}, u32[]{:S(2)}) collective-permute-start(bf16[1,144,256]{2,1,0:T(8,128)(2,1)} %get-tuple-element.115), channel_id=1, source_target_pairs={{0,8},{2,10},{4,12},{6,14},{8,16},{10,18},{12,20},{14,22},{16,24},... | collective-permute-start | bytes 221192 | tf_op jit(solution)/shard_map/ppermute | solution.py:177
  4.7 1.1 %collective-permute-start.2 = (bf16[1,144,256]{2,1,0:T(8,128)(2,1)}, bf16[1,144,256]{2,1,0:T(8,128)(2,1)S(1)}, u32[]{:S(2)}, u32[]{:S(2)}) collective-permute-start(bf16[1,144,256]{2,1,0:T(8,128)(2,1)} %get-tuple-element.116), channel_id=1, source_target_pairs={{0,16},{2,18},{4,20},{6,22},{8,24},{10,26},{12,28},{14,30},{16,0},... | collective-permute-start | bytes 221192 | tf_op jit(solution)/shard_map/ppermute | solution.py:177
  5.8 1.4 %collective-permute-start.3 = (bf16[1,144,256]{2,1,0:T(8,128)(2,1)}, bf16[1,144,256]{2,1,0:T(8,128)(2,1)S(1)}, u32[]{:S(2)}, u32[]{:S(2)}) collective-permute-start(bf16[1,144,256]{2,1,0:T(8,128)(2,1)} %get-tuple-element.117), channel_id=1, source_target_pairs={{0,24},{2,26},{4,28},{6,30},{8,0},{10,2},{12,4},{14,6},{16,8},{18,... | collective-permute-start | bytes 221192 | tf_op jit(solution)/shard_map/ppermute | solution.py:177
  7.1 0.0 copy-start.3
  7.1 0.0 copy-start.2
  7.1 0.0 copy-start.1
  7.1 4.7 %all-to-all-start.1 = ((bf16[16,2,128,256]{3,2,1,0:T(8,128)(2,1)}), bf16[16,2,128,256]{3,2,1,0:T(8,128)(2,1)S(1)}, u32[]{:S(2)}, u32[]{:S(2)}) async-start(bf16[16,2,128,256]{3,2,1,0:T(8,128)(2,1)} %bitcast.17), calls=%async_computation.1 | async-start | bytes 4194304 | tf_op jit(solution)/shard_map/all_to_all | solution.py:627
  11.8 0.0 copy-done.3
  11.8 0.1 reduce_sum.9
  12.0 0.1 divide_convert_fusion
  12.0 0.0 copy-done.2
  12.1 0.7 stack.44.shifts
  12.8 0.5 fusion.5.source
  13.3 0.0 collective-permute-done.1
  13.3 0.0 collective-permute-done.2
  13.3 0.0 collective-permute-done.3
  13.3 1.2 %collective-permute-start.4 = (bf16[4,144,256]{2,1,0:T(8,128)(2,1)S(1)}, bf16[4,144,256]{2,1,0:T(8,128)(2,1)}, u32[]{:S(2)}, u32[]{:S(2)}) collective-permute-start(bf16[4,144,256]{2,1,0:T(8,128)(2,1)S(1)} %constant_dynamic-update-slice_fusion.refs_0_), channel_id=1, source_target_pairs={{0,2},{2,0},{4,6},{6,4},{8,10},{10,8},{12,14},{14,12},{16,18},{18,... | collective-permute-start | bytes 884744 | tf_op jit(solution)/shard_map/ppermute | solution.py:188
  14.6 0.3 collective-permute-start.5
  14.9 1.2 %collective-permute-start.6 = (bf16[4,144,256]{2,1,0:T(8,128)(2,1)S(1)}, bf16[4,144,256]{2,1,0:T(8,128)(2,1)}, u32[]{:S(2)}, u32[]{:S(2)}) collective-permute-start(bf16[4,144,256]{2,1,0:T(8,128)(2,1)S(1)} %constant_dynamic-update-slice_fusion.refs_0_), channel_id=1, source_target_pairs={{0,6},{2,4},{4,2},{6,0},{8,14},{10,12},{12,10},{14,8},{16,22},{18,... | collective-permute-start | bytes 884744 | tf_op jit(solution)/shard_map/ppermute | solution.py:188
  16.1 0.1 rev.3
  16.1 0.0 copy-done.1
  16.2 3.0 %collective-permute-start.7 = (f32[4,64,256]{2,1,0:T(8,128)S(1)}, f32[4,64,256]{2,1,0:T(8,128)S(1)}, u32[]{:S(2)}, u32[]{:S(2)}) collective-permute-start(f32[4,64,256]{2,1,0:T(8,128)S(1)} %constant_dynamic-slice_fusion.2), channel_id=1, source_target_pairs={{0,1},{1,0},{2,3},{3,2},{4,5},{5,4},{6,7},{7,6},{8,9},{9,8},{10,11... | collective-permute-start | bytes 786440 | tf_op jit(solution)/shard_map/ppermute | solution.py:248
  19.1 0.6 fusion.3.taps_rows
  19.8 6.1 %bands.1 = (bf16[6,176,192]{2,1,0:T(8,128)(2,1)}, bf16[6,160,176]{2,1,0:T(8,128)(2,1)}, bf16[6,144,160]{2,1,0:T(8,128)(2,1)}, bf16[6,128,144]{2,1,0:T(8,128)(2,1)}) custom-call(s32[8]{0:T(128)} %stack.44.shifts, f32[2,6,256]{2,1,0:T(8,128)} %fusion.3.taps_rows), custom_call_target="tpu_custom_call" | custom-call | flops 99999997952 | tf_op jit(solution)/shard_map/bands/pallas_call | solution.py:336
  25.9 0.0 collective-permute-done.7
  25.9 1.3 %maximum_select_fusion = f32[4,192,256]{2,1,0:T(8,128)S(1)} fusion(f32[4,64,256]{2,1,0:T(8,128)S(1)} %collective-permute-done.7, f32[4,128,256]{2,1,0:T(8,128)} %param.7, pred[]{:T(512)S(6)} %eq.4), kind=kLoop, calls=%fused_computation.1 | loop fusion | flops 589824 | bytes 1572865 | tf_op jit(solution)/shard_map/jit(_where)/select_n | solution.py:262
  27.2 0.0 collective-permute-done.4.refs_1_
  27.2 10.9 %collective-permute-done.5.refs_2_ = bf16[4,144,256]{2,1,0:T(8,128)(2,1)} collective-permute-done((bf16[4,144,256]{2,1,0:T(8,128)(2,1)S(1)}, bf16[4,144,256]{2,1,0:T(8,128)(2,1)}, u32[]{:S(2)}, u32[]{:S(2)}) %collective-permute-start.5) | collective-permute-done | bytes 294944 | tf_op jit(solution)/shard_map/ppermute | solution.py:188
  38.1 0.0 collective-permute-done.6.refs_3_
  38.1 0.0 copy-start.4
  38.1 1.8 %ends.1 = bf16[16,48,256]{2,1,0:T(8,128)(2,1)} custom-call(s32[1]{0:T(128)} %bitcast.10.start, bf16[4,144,256]{2,1,0:T(8,128)(2,1)S(1)} %constant_dynamic-update-slice_fusion.refs_0_, bf16[4,144,256]{2,1,0:T(8,128)(2,1)} %collective-permute-done.4.refs_1_, bf16[4,144,256]{2,1,0:T(8,128)(2,1)} %collective-permute-done.5.refs_2_, ...), custom_call_target="tpu_custom_call" | custom-call | tf_op jit(solution)/shard_map/ends/pallas_call | solution.py:229
  39.9 4.1 %collective-permute-start.8 = (bf16[16,48,256]{2,1,0:T(8,128)(2,1)}, bf16[16,48,256]{2,1,0:T(8,128)(2,1)}, u32[]{:S(2)}, u32[]{:S(2)}) collective-permute-start(bf16[16,48,256]{2,1,0:T(8,128)(2,1)} %ends.1), channel_id=1, source_target_pairs={{0,1},{1,0},{2,3},{3,2},{4,5},{5,4},{6,7},{7,6},{8,9},{9,8},{10,11... | collective-permute-start | bytes 1179656 | tf_op jit(solution)/shard_map/ppermute | solution.py:248
  44.0 0.6 pad_add_fusion.place
  44.6 4.1 %plan.1 = (s32[279]{0:T(512)S(1)}, s32[1]{0:T(128)}) custom-call(s32[2]{0:T(128)} %pad_add_fusion.place, s32[16]{0:T(128)} %fusion.5.source, bf16[4,144,256]{2,1,0:T(8,128)(2,1)S(1)} %constant_dynamic-update-slice_fusion.refs_0_, bf16[4,144,256]{2,1,0:T(8,128)(2,1)} %collective-permute-done.4.refs_1_, bf16[4,144,256]{2,1,0:T(8,128)(2,1)} %collective-permute-done.5.refs_2_, ...), custom_call_target="tpu_custom_call" | custom-call | tf_op jit(solution)/shard_map/plan/pallas_call | solution.py:422
  48.7 0.0 collective-permute-done.8
  48.7 11.3 %all-to-all-done.1 = bf16[16,2,128,256]{3,2,1,0:T(8,128)(2,1)S(1)} async-done(((bf16[16,2,128,256]{3,2,1,0:T(8,128)(2,1)}), bf16[16,2,128,256]{3,2,1,0:T(8,128)(2,1)S(1)}, u32[]{:S(2)}, u32[]{:S(2)}) %all-to-all-start.1) | async-done | bytes 2097184 | tf_op jit(solution)/shard_map/all_to_all | solution.py:627
  60.0 0.1 constant_dynamic-slice_fusion.1
  60.0 1.6 %collective-permute-start.9 = (bf16[32,48,256]{2,1,0:T(8,128)(2,1)S(1)}, bf16[32,48,256]{2,1,0:T(8,128)(2,1)}, u32[]{:S(2)}, u32[]{:S(2)}) collective-permute-start(bf16[32,48,256]{2,1,0:T(8,128)(2,1)S(1)} %constant_dynamic-slice_fusion.1), channel_id=1, source_target_pairs={{0,1},{1,0},{2,3},{3,2},{4,5},{5,4},{6,7},{7,6},{8,9},{9,8},{10,11... | collective-permute-start | bytes 2359304 | tf_op jit(solution)/shard_map/ppermute | solution.py:248
  62.3 1.3 %collective-permute-done.9 = bf16[32,48,256]{2,1,0:T(8,128)(2,1)} collective-permute-done((bf16[32,48,256]{2,1,0:T(8,128)(2,1)S(1)}, bf16[32,48,256]{2,1,0:T(8,128)(2,1)}, u32[]{:S(2)}, u32[]{:S(2)}) %collective-permute-start.9) | collective-permute-done | bytes 786464 | tf_op jit(solution)/shard_map/ppermute | solution.py:248
  63.6 0.0 copy-done.4
  63.6 5.6 %conditional.1 = (f32[4,128,256]{2,1,0:T(8,128)}) conditional(s32[]{:T(128)} %bitcast.13, (s32[279]{0:T(512)S(1)}, bf16[32,128,256]{2,1,0:T(8,128)(2,1)S(1)}, f32[4,192,256]{2,1,0:T(8,128)S(1)}, bf16[4,144,256]{2,1,0:T(8,128)(2,1)S(1)}, bf16[4,144,256]{2,1,0:T(8,128)(2,1)}, /*index=5*/bf16[4,144,256]{2,1,0:T(8,128)(2,1)}, ...), branch_computations={%region_1.2_spmd, %region_2.3_spmd} | conditional | flops 4 | bytes 8650906 | solution.py:668
  63.6 5.4 %deconvolve.2 = f32[4,128,256]{2,1,0:T(8,128)} custom-call(s32[279]{0:T(512)S(1)} %get-tuple-element.54.listed, bf16[32,128,256]{2,1,0:T(8,128)(2,1)S(1)} %get-tuple-element.55.main, f32[4,192,256]{2,1,0:T(8,128)S(1)} %get-tuple-element.56.est, bf16[4,144,256]{2,1,0:T(8,128)(2,1)S(1)} %get-tuple-element.57.refs_0_, ...), custom_call_target="tpu_custom_call" | custom-call | tf_op jit(solution)/shard_map/cond/branch_0_fun/deconvolve/pallas_call | solution.py:588
  (5 shorter events, 0.0 us)
Async XLA Ops:
  3.3 10.0 %collective-permute-start.1 = (bf16[1,144,256]{2,1,0:T(8,128)(2,1)}, bf16[1,144,256]{2,1,0:T(8,128)(2,1)S(1)}, u32[]{:S(2)}, u32[]{:S(2)}) collective-permute-start(bf16[1,144,256]{2,1,0:T(8,128)(2,1)} %get-tuple-element.115), channel_id=1, source_target_pairs={{0,8},{2,10},{4,12},{6,14},{8,16},{10,18},{12,20},{14,22},{16,24},... | collective-permute-start | bytes 221192 | tf_op jit(solution)/shard_map/ppermute | solution.py:177
  4.7 8.6 %collective-permute-start.2 = (bf16[1,144,256]{2,1,0:T(8,128)(2,1)}, bf16[1,144,256]{2,1,0:T(8,128)(2,1)S(1)}, u32[]{:S(2)}, u32[]{:S(2)}) collective-permute-start(bf16[1,144,256]{2,1,0:T(8,128)(2,1)} %get-tuple-element.116), channel_id=1, source_target_pairs={{0,16},{2,18},{4,20},{6,22},{8,24},{10,26},{12,28},{14,30},{16,0},... | collective-permute-start | bytes 221192 | tf_op jit(solution)/shard_map/ppermute | solution.py:177
  5.8 7.6 %collective-permute-start.3 = (bf16[1,144,256]{2,1,0:T(8,128)(2,1)}, bf16[1,144,256]{2,1,0:T(8,128)(2,1)S(1)}, u32[]{:S(2)}, u32[]{:S(2)}) collective-permute-start(bf16[1,144,256]{2,1,0:T(8,128)(2,1)} %get-tuple-element.117), channel_id=1, source_target_pairs={{0,24},{2,26},{4,28},{6,30},{8,0},{10,2},{12,4},{14,6},{16,8},{18,... | collective-permute-start | bytes 221192 | tf_op jit(solution)/shard_map/ppermute | solution.py:177
  7.1 4.7 %copy-start.3 = (f32[6,33]{1,0:T(8,128)S(1)}, f32[6,33]{1,0:T(8,128)}, u32[]{:S(2)}) copy-start(f32[6,33]{1,0:T(8,128)} %param.11) | copy-start | bytes 2380
  7.1 4.9 %copy-start.2 = (bf16[1,144,256]{2,1,0:T(8,128)(2,1)S(1)}, bf16[1,144,256]{2,1,0:T(8,128)(2,1)}, u32[]{:S(2)}) copy-start(bf16[1,144,256]{2,1,0:T(8,128)(2,1)} %get-tuple-element.114) | copy-start | bytes 221188
  7.1 9.0 %copy-start.1 = (f32[4,128,256]{2,1,0:T(8,128)S(1)}, f32[4,128,256]{2,1,0:T(8,128)}, u32[]{:S(2)}) copy-start(f32[4,128,256]{2,1,0:T(8,128)} %param.7) | copy-start | bytes 1572868
  7.1 52.8 %all-to-all-start.1 = ((bf16[16,2,128,256]{3,2,1,0:T(8,128)(2,1)}), bf16[16,2,128,256]{3,2,1,0:T(8,128)(2,1)S(1)}, u32[]{:S(2)}, u32[]{:S(2)}) async-start(bf16[16,2,128,256]{3,2,1,0:T(8,128)(2,1)} %bitcast.17), calls=%async_computation.1 | async-start | bytes 4194304 | tf_op jit(solution)/shard_map/all_to_all | solution.py:627
  13.3 13.8 %collective-permute-start.4 = (bf16[4,144,256]{2,1,0:T(8,128)(2,1)S(1)}, bf16[4,144,256]{2,1,0:T(8,128)(2,1)}, u32[]{:S(2)}, u32[]{:S(2)}) collective-permute-start(bf16[4,144,256]{2,1,0:T(8,128)(2,1)S(1)} %constant_dynamic-update-slice_fusion.refs_0_), channel_id=1, source_target_pairs={{0,2},{2,0},{4,6},{6,4},{8,10},{10,8},{12,14},{14,12},{16,18},{18,... | collective-permute-start | bytes 884744 | tf_op jit(solution)/shard_map/ppermute | solution.py:188
  14.6 23.5 %collective-permute-start.5 = (bf16[4,144,256]{2,1,0:T(8,128)(2,1)S(1)}, bf16[4,144,256]{2,1,0:T(8,128)(2,1)}, u32[]{:S(2)}, u32[]{:S(2)}) collective-permute-start(bf16[4,144,256]{2,1,0:T(8,128)(2,1)S(1)} %constant_dynamic-update-slice_fusion.refs_0_), channel_id=1, source_target_pairs={{0,4},{2,6},{4,0},{6,2},{8,12},{10,14},{12,8},{14,10},{16,20},{18,... | collective-permute-start | bytes 884744 | tf_op jit(solution)/shard_map/ppermute | solution.py:188
  14.9 23.2 %collective-permute-start.6 = (bf16[4,144,256]{2,1,0:T(8,128)(2,1)S(1)}, bf16[4,144,256]{2,1,0:T(8,128)(2,1)}, u32[]{:S(2)}, u32[]{:S(2)}) collective-permute-start(bf16[4,144,256]{2,1,0:T(8,128)(2,1)S(1)} %constant_dynamic-update-slice_fusion.refs_0_), channel_id=1, source_target_pairs={{0,6},{2,4},{4,2},{6,0},{8,14},{10,12},{12,10},{14,8},{16,22},{18,... | collective-permute-start | bytes 884744 | tf_op jit(solution)/shard_map/ppermute | solution.py:188
  16.2 9.7 %collective-permute-start.7 = (f32[4,64,256]{2,1,0:T(8,128)S(1)}, f32[4,64,256]{2,1,0:T(8,128)S(1)}, u32[]{:S(2)}, u32[]{:S(2)}) collective-permute-start(f32[4,64,256]{2,1,0:T(8,128)S(1)} %constant_dynamic-slice_fusion.2), channel_id=1, source_target_pairs={{0,1},{1,0},{2,3},{3,2},{4,5},{5,4},{6,7},{7,6},{8,9},{9,8},{10,11... | collective-permute-start | bytes 786440 | tf_op jit(solution)/shard_map/ppermute | solution.py:248
  38.1 25.5 %copy-start.4 = (s32[4,6]{1,0:T(4,128)S(1)}, s32[4,6]{1,0:T(4,128)}, u32[]{:S(2)}) copy-start(s32[4,6]{1,0:T(4,128)} %owners.1) | copy-start | bytes 292
  39.9 8.8 %collective-permute-start.8 = (bf16[16,48,256]{2,1,0:T(8,128)(2,1)}, bf16[16,48,256]{2,1,0:T(8,128)(2,1)}, u32[]{:S(2)}, u32[]{:S(2)}) collective-permute-start(bf16[16,48,256]{2,1,0:T(8,128)(2,1)} %ends.1), channel_id=1, source_target_pairs={{0,1},{1,0},{2,3},{3,2},{4,5},{5,4},{6,7},{7,6},{8,9},{9,8},{10,11... | collective-permute-start | bytes 1179656 | tf_op jit(solution)/shard_map/ppermute | solution.py:248
  60.0 3.6 %collective-permute-start.9 = (bf16[32,48,256]{2,1,0:T(8,128)(2,1)S(1)}, bf16[32,48,256]{2,1,0:T(8,128)(2,1)}, u32[]{:S(2)}, u32[]{:S(2)}) collective-permute-start(bf16[32,48,256]{2,1,0:T(8,128)(2,1)S(1)} %constant_dynamic-slice_fusion.1), channel_id=1, source_target_pairs={{0,1},{1,0},{2,3},{3,2},{4,5},{5,4},{6,7},{7,6},{8,9},{9,8},{10,11... | collective-permute-start | bytes 2359304 | tf_op jit(solution)/shard_map/ppermute | solution.py:248
